TPU v7x, 32 devices: a whole 2x2x4 slice. The times are simulated.
32 devices in a mesh: pipe: 4 (over z), tensor: 4 (over y, core), dp: 2 (over x).
Axes of the slice: x: 2, y: 2, z: 4, core: 2. Of those that a mesh axis runs over, the one named last changes fastest.
Arguments:
- query_heads: bfloat16 [8, 512, 4096], P(('dp', 'pipe'), None, 'tensor'), parts along dimension 0, may hold values from -5 to 5, as said below
- key_heads: bfloat16 [8, 512, 4096], P(('dp', 'pipe'), None, 'tensor'), parts along dimension 0, may hold values from -5 to 5
- value_heads: bfloat16 [8, 512, 4096], P(('dp', 'pipe'), None, 'tensor'), parts along dimension 0, may hold values from -16 to 16
- segment_ids: int32 [8, 512], P(('dp', 'pipe')), parts along dimension 0, may hold values from 0 to 3, never falling along the last dimension, each value on 1 to 256 neighbouring positions
- section_input: bfloat16 [8, 512, 8192], P(('dp', 'pipe'), 'tensor'), parts along dimension 0, may hold values from -6 to 6
- out_weight: bfloat16 [8, 4096, 8192], P(('dp', 'pipe'), 'tensor'), parts along dimension 0, may hold values from -0.1875 to 0.1875
Outputs:
- received: bfloat16 [8, 512, 8192], P(('dp', 'pipe'), 'tensor'), parts along dimension 0
- evicted: bfloat16 [8, 512, 8192], P(('dp', 'pipe'), 'tensor'), parts along dimension 0
- evicted_scale: float32 [8, 512], P(('dp', 'pipe'), 'tensor'), parts along dimension 0
There are 2 independent parts, one for each index of `dp`. A program takes and returns all parts, laid end to end along the dimension named above; each array names one. Nothing has to cross between parts.
Inputs may be any that keep to these rules, and one draw needn't show every extreme that they name: `query_heads`: queries and keys are bfloat16 values of moderate size. `segment_ids`: each section's segment numbers never fall along the tokens; every document is 1 to 256 tokens long.
All inputs are finite; a program needn't handle non-finite values. Where the computation divides by a largest or mean magnitude, that divisor is 1e-20 or more.
Results may differ from a plain program's by a relative error of at most 0.0055.
Values may be sent and summed in bfloat16 or wider, within the bound.
No kernel may reach another device: no remote copies, remote signals or barrier semaphores. Data moves between devices by JAX's collectives and lax.ppermute only.
A program may use at most 128 MiB of HBM per device.

v0:
```python
import math

import jax
import jax.numpy as jnp
from jax import lax
from jax.sharding import PartitionSpec as P

HD = 128


def shifted(value, axis, steps):
    count = lax.axis_size(axis)
    leading, last = (max(0, -steps), min(count, count - steps))
    return lax.ppermute(value, axis, [(source, source + steps) for source in range(leading, last)])


def from_partner(value, axis, apart):
    mask = 2**apart
    pairs = [(source, source ^ mask) for source in range(lax.axis_size(axis))]
    return lax.ppermute(value, axis, pairs)


def per_device(query_heads, key_heads, value_heads, segment_ids, section_input, out_weight):
    query_block = query_heads[0]
    key_block = key_heads[0]
    value_block = value_heads[0]
    segment_row = segment_ids[0]
    input_block = section_input[0]
    weight_block = out_weight[0]
    row_count = query_block.shape[0]
    head_count = query_block.shape[1] // HD
    query_three = query_block.reshape(row_count, head_count, HD)
    key_three = key_block.reshape(row_count, head_count, HD)
    value_three = value_block.reshape(row_count, head_count, HD)
    position = jnp.arange(row_count, dtype=jnp.int32)
    allowed = (segment_row[:, None] == segment_row[None, :]) & (
        position[None, :] <= position[:, None]
    )
    scores = jnp.einsum(
        "qhd,khd->hqk", query_three, key_three, preferred_element_type=jnp.float32
    ) * (1.0 / math.sqrt(HD))
    scores = jnp.where(allowed[None, :, :], scores, jnp.float32(-1e30))
    row_max = jnp.max(scores, axis=2, keepdims=True)
    expons = jnp.exp(scores - row_max)
    weights = (expons / jnp.sum(expons, axis=2, keepdims=True)).astype(jnp.bfloat16)
    heads_out = jnp.einsum("hqk,khd->qhd", weights, value_three, preferred_element_type=jnp.float32)
    heads_out = heads_out.astype(jnp.bfloat16).reshape(row_count, head_count * HD)
    wide_input = input_block.astype(jnp.float32)
    scale = jnp.max(jnp.abs(wide_input), axis=1) + 1e-06
    packed = (wide_input / scale[:, None]).astype(jnp.bfloat16)
    partial_value = jnp.dot(heads_out, weight_block, preferred_element_type=jnp.float32)
    mine = lax.psum_scatter(partial_value, "tensor", scatter_dimension=0, tiled=True)
    section_out = (wide_input + mine).astype(jnp.bfloat16)
    received = shifted(section_out[None], "pipe", 1)
    bit_total = lax.axis_size("pipe").bit_length() - 1
    moving = (packed[None], scale[None])
    for bit_index in range(bit_total):
        moving = (
            from_partner(moving[0], "pipe", bit_index),
            from_partner(moving[1].astype(jnp.bfloat16), "pipe", bit_index).astype(jnp.float32),
        )
    evicted, evicted_scale = moving
    return (received, evicted, evicted_scale)


def solution(mesh):
    return jax.shard_map(
        per_device,
        mesh=mesh,
        in_specs=(
            P(("dp", "pipe"), None, "tensor"),
            P(("dp", "pipe"), None, "tensor"),
            P(("dp", "pipe"), None, "tensor"),
            P(("dp", "pipe"), None),
            P(("dp", "pipe"), "tensor", None),
            P(("dp", "pipe"), "tensor", None),
        ),
        out_specs=(
            P(("dp", "pipe"), "tensor", None),
            P(("dp", "pipe"), "tensor", None),
            P(("dp", "pipe"), "tensor"),
        ),
        check_vma=False,
    )
```

profile of v0, /device:TPU:16, one launch (start us, length us, event | category | flops | bytes accessed | tf_op | source)
XLA Modules:
  0.0 317.2 jit_solution(9340930804246003919)
XLA Ops:
  7.2 0.0 reduce-scatter.2.cloned.1.call-start
  7.2 1.0 fusion.18
  8.2 1.5 copy.15
  9.7 1.5 copy.16
  11.2 2.3 copy.14
  13.5 1.3 fusion.15
  14.7 0.0 copy-start.1
  14.7 0.0 slice-start
  14.7 0.0 slice-start.1
  14.8 5.7 %fusion.21 = (f32[8,512]{1,0:T(8,128)S(1)}, f32[8,512,512]{1,2,0:T(8,128)}) fusion(f32[8,512,512]{1,2,0:T(8,128)S(1)} %fusion.15, pred[512,512]{0,1:T(8,128)(4,1)S(1)} %fusion.18), kind=kOutput, calls=%fused_computation.29 | output fusion | flops 12583423 | bytes 17055744 | tf_op jit(solution)/shard_map/sub | solution.py:44
  20.4 0.0 copy-done.1
  20.5 4.3 %fusion.14 = bf16[8,512,128]{1,2,0:T(8,128)(2,1)S(1)} fusion(bf16[512,8,128]{0,2,1:T(8,128)(2,1)S(1)} %bitcast.39, f32[8,512,512]{1,2,0:T(8,128)} %get-tuple-element.8, f32[8,512]{1,0:T(8,128)S(1)} %get-tuple-element.7), kind=kOutput, calls=%fused_computation.19 | convolution fusion | flops 541589504 | bytes 10502144 | tf_op jit(solution)/shard_map/hqk,khd->qhd/dot_general | solution.py:46
  24.7 0.3 slice-done.2
  25.1 1.2 slice-done.3
  26.3 11.7 %fusion.1 = f32[512,8192]{1,0:T(8,128)} fusion(bf16[512,1024]{0,1:T(8,128)(2,1)S(1)} %bitcast.34, bf16[1,1024,8192]{2,1,0:T(8,128)(2,1)S(1)} %bitcast.33), kind=kOutput, calls=%fused_computation.1 | convolution fusion | flops 8589934592 | bytes 34603008 | tf_op jit(solution)/shard_map/dot_general | solution.py:51
  38.0 0.0 reduce-scatter.2.cloned.1.call-update
  38.0 127.3 %reduce-scatter.2.cloned.1.call-done = f32[128,8192]{1,0:T(8,128)} async-done(((f32[512,8192]{1,0:T(8,128)}), f32[128,8192]{1,0:T(8,128)}) %reduce-scatter.2.cloned.1.call-update) | async-done | bytes 4194320 | tf_op jit(solution)/shard_map/reduce_scatter | solution.py:52
  165.3 2.9 fusion.7
  168.2 0.5 fusion.8
  168.7 1.6 collective-permute-start.1
  170.3 2.4 collective-permute-start
  172.7 43.6 %collective-permute-done.1 = bf16[1,128,8192]{2,1,0:T(8,128)(2,1)S(1)} collective-permute-done((bf16[1,128,8192]{2,1,0:T(8,128)(2,1)S(1)}, bf16[1,128,8192]{2,1,0:T(8,128)(2,1)S(1)}, u32[]{:S(2)}, u32[]{:S(2)}) %collective-permute-start.1) | collective-permute-done | bytes 2097184 | tf_op jit(solution)/shard_map/ppermute | solution.py:20
  216.3 0.5 collective-permute-start.2
  216.8 2.5 collective-permute-start.3
  219.3 82.7 %collective-permute-done.3 = bf16[1,128]{1,0:T(2,128)(2,1)S(1)} collective-permute-done((bf16[1,128]{1,0:T(2,128)(2,1)S(1)}, bf16[1,128]{1,0:T(2,128)(2,1)S(1)}, u32[]{:S(2)}, u32[]{:S(2)}) %collective-permute-start.3) | collective-permute-done | bytes 288 | tf_op jit(solution)/shard_map/ppermute | solution.py:20
  302.1 3.6 %collective-permute-start.4 = (bf16[1,128]{1,0:T(2,128)(2,1)S(1)}, bf16[1,128]{1,0:T(2,128)(2,1)S(1)}, u32[]{:S(2)}, u32[]{:S(2)}) collective-permute-start(bf16[1,128]{1,0:T(2,128)(2,1)S(1)} %collective-permute-done.3), channel_id=1, source_target_pairs={{0,16},{8,24},{16,0},{24,8},{1,17},{9,25},{17,1},{25,9},{2,18},{10... | collective-permute-start | bytes 776 | tf_op jit(solution)/shard_map/ppermute | solution.py:20
  305.7 1.5 collective-permute-done.4
  307.2 0.5 convert_element_type.54
  307.7 0.0 collective-permute-done
  307.7 0.0 collective-permute-done.2
  307.7 1.3 copy.23
  309.0 1.3 copy.24
  (8 shorter events, 0.0 us)
Async XLA Ops:
  7.2 158.1 %reduce-scatter.2.cloned.1.call-start = ((), (), s32[]{:S(2)}) async-start(), calls=%async_computation.1 | async-start | bytes 20971520 | tf_op jit(solution)/shard_map/reduce_scatter | solution.py:52
  14.7 5.7 %copy-start.1 = (bf16[1,512,1024]{1,2,0:T(8,128)(2,1)S(1)}, bf16[1,512,1024]{1,2,0:T(8,128)(2,1)}, u32[]{:S(2)}) copy-start(bf16[1,512,1024]{1,2,0:T(8,128)(2,1)} %copy.14) | copy-start | bytes 3145732
  14.7 10.0 %slice-start = ((s8[16777216]{0:T(1024)(128)(4,1)}), s8[4194304]{0:T(1024)(128)(4,1)S(1)}, s32[]{:S(2)}) async-start(s8[16777216]{0:T(1024)(128)(4,1)} %bitcast.32), calls=%async_computation.2 | async-start | bytes 8388608
  14.7 10.0 %slice-start.1 = ((s8[16777216]{0:T(1024)(128)(4,1)}), s8[4194304]{0:T(1024)(128)(4,1)S(1)}, s32[]{:S(2)}) async-start(s8[16777216]{0:T(1024)(128)(4,1)} %bitcast.32), calls=%async_computation.3 | async-start | bytes 8388608
  20.4 4.6 %slice-start.2 = ((s8[16777216]{0:T(1024)(128)(4,1)}), s8[4194304]{0:T(1024)(128)(4,1)S(1)}, s32[]{:S(2)}) async-start(s8[16777216]{0:T(1024)(128)(4,1)} %bitcast.32), calls=%async_computation.4 | async-start | bytes 8388608
  20.5 5.8 %slice-start.3 = ((s8[16777216]{0:T(1024)(128)(4,1)}), s8[4194304]{0:T(1024)(128)(4,1)S(1)}, s32[]{:S(2)}) async-start(s8[16777216]{0:T(1024)(128)(4,1)} %bitcast.32), calls=%async_computation.5 | async-start | bytes 8388608
  38.0 127.3 %copy-start = (bf16[1,128,8192]{2,1,0:T(8,128)(2,1)S(1)}, bf16[1,128,8192]{2,1,0:T(8,128)(2,1)}, u32[]{:S(2)}) copy-start(bf16[1,128,8192]{2,1,0:T(8,128)(2,1)} %param.10) | copy-start | bytes 6291460
  168.7 47.6 %collective-permute-start.1 = (bf16[1,128,8192]{2,1,0:T(8,128)(2,1)S(1)}, bf16[1,128,8192]{2,1,0:T(8,128)(2,1)S(1)}, u32[]{:S(2)}, u32[]{:S(2)}) collective-permute-start(bf16[1,128,8192]{2,1,0:T(8,128)(2,1)S(1)} %fusion.8), channel_id=1, source_target_pairs={{0,8},{8,0},{16,24},{24,16},{1,9},{9,1},{17,25},{25,17},{2,10},{10... | collective-permute-start | bytes 6291464 | tf_op jit(solution)/shard_map/ppermute | solution.py:20
  170.3 137.4 %collective-permute-start = (bf16[1,128,8192]{2,1,0:T(8,128)(2,1)S(1)}, bf16[1,128,8192]{2,1,0:T(8,128)(2,1)S(1)}, u32[]{:S(2)}, u32[]{:S(2)}) collective-permute-start(bf16[1,128,8192]{2,1,0:T(8,128)(2,1)S(1)} %get-tuple-element.4), channel_id=1, source_target_pairs={{0,8},{8,16},{16,24},{1,9},{9,17},{17,25},{2,10},{10,18},{18,26},{... | collective-permute-start | bytes 6291464 | tf_op jit(solution)/shard_map/ppermute | solution.py:14
  216.3 91.4 %collective-permute-start.2 = (bf16[1,128,8192]{2,1,0:T(8,128)(2,1)S(1)}, bf16[1,128,8192]{2,1,0:T(8,128)(2,1)S(1)}, u32[]{:S(2)}, u32[]{:S(2)}) collective-permute-start(bf16[1,128,8192]{2,1,0:T(8,128)(2,1)S(1)} %collective-permute-done.1), channel_id=1, source_target_pairs={{0,16},{8,24},{16,0},{24,8},{1,17},{9,25},{17,1},{25,9},{2,18},{10... | collective-permute-start | bytes 6291464 | tf_op jit(solution)/shard_map/ppermute | solution.py:20
  216.8 85.2 %collective-permute-start.3 = (bf16[1,128]{1,0:T(2,128)(2,1)S(1)}, bf16[1,128]{1,0:T(2,128)(2,1)S(1)}, u32[]{:S(2)}, u32[]{:S(2)}) collective-permute-start(bf16[1,128]{1,0:T(2,128)(2,1)S(1)} %get-tuple-element.5), channel_id=1, source_target_pairs={{0,8},{8,0},{16,24},{24,16},{1,9},{9,1},{17,25},{25,17},{2,10},{10... | collective-permute-start | bytes 776 | tf_op jit(solution)/shard_map/ppermute | solution.py:20
  302.1 5.1 %collective-permute-start.4 = (bf16[1,128]{1,0:T(2,128)(2,1)S(1)}, bf16[1,128]{1,0:T(2,128)(2,1)S(1)}, u32[]{:S(2)}, u32[]{:S(2)}) collective-permute-start(bf16[1,128]{1,0:T(2,128)(2,1)S(1)} %collective-permute-done.3), channel_id=1, source_target_pairs={{0,16},{8,24},{16,0},{24,8},{1,17},{9,25},{17,1},{25,9},{2,18},{10... | collective-permute-start | bytes 776 | tf_op jit(solution)/shard_map/ppermute | solution.py:20
Sparse Core Ops, SparseCore 0:
  38.1 127.1 reduce-scatter.1
where the time goes:
time: 322 us; the launch traced here: 317 us
  waiting for transfers between devices  255 us (79%)
  matrix products  17.2 us (5%)
  between operations  14.1 us (4%)
  starting transfers between devices  10.7 us (3%)
  other arithmetic  10.6 us (3%)
  local copies, waits for them, and re-layouts  9.45 us (3%)
    ppermute x4, waiting for transfers between devices, from_partner(): return lax.ppermute(value, axis, pairs)  128 us
    reduce_scatter x1, waiting for transfers between devices, per_device(): lax.psum_scatter(partial_value, 'tensor', scatter_dimension=0, tiled=True)  127 us
    dot_general x1, matrix products, per_device(): jnp.dot(heads_out, weight_block, preferred_element_type=jnp.float32)  11.7 us
    ppermute x4, starting transfers between devices, from_partner(): return lax.ppermute(value, axis, pairs)  8.19 us
    unnamed x16, local copies, waits for them, and re-layouts  7.17 us
  transfers between devices with their start and end apart: 6, of which 4 were waited for; matrix products, arithmetic and copies ran while one was open for 0% of the time, Pallas kernels for 0%

commit v1 on v0

v1 whole, which is shorter than its diff:
```python
import math

import jax
import jax.numpy as jnp
from jax import lax
from jax.sharding import PartitionSpec as P

HD = 128
CHUNKS = 4


def attention(query_block, key_block, value_block, segment_row):
    row_count = query_block.shape[0]
    head_count = query_block.shape[1] // HD
    query_three = query_block.reshape(row_count, head_count, HD)
    key_three = key_block.reshape(row_count, head_count, HD)
    value_three = value_block.reshape(row_count, head_count, HD)
    position = jnp.arange(row_count, dtype=jnp.int32)
    allowed = (segment_row[:, None] == segment_row[None, :]) & (
        position[None, :] <= position[:, None]
    )
    scores = jnp.einsum(
        "qhd,khd->hqk", query_three, key_three, preferred_element_type=jnp.float32
    ) * (1.0 / math.sqrt(HD))
    scores = jnp.where(allowed[None, :, :], scores, jnp.float32(-1e30))
    row_max = jnp.max(scores, axis=2, keepdims=True)
    expons = jnp.exp(scores - row_max)
    weights = (expons / jnp.sum(expons, axis=2, keepdims=True)).astype(jnp.bfloat16)
    heads_out = jnp.einsum("hqk,khd->qhd", weights, value_three, preferred_element_type=jnp.float32)
    return heads_out.astype(jnp.bfloat16).reshape(row_count, head_count * HD)


def scattered_sum(heads_out, weight, axis):
    count = lax.axis_size(axis)
    bits = count.bit_length() - 1
    index = lax.axis_index(axis)
    rows, depth = heads_out.shape
    owned = heads_out.reshape((2,) * bits + (rows // count, depth))
    low = index & 1
    theirs = lax.dynamic_index_in_dim(owned, 1 - low, axis=bits - 1, keepdims=False)
    mine = lax.dynamic_index_in_dim(owned, low, axis=bits - 1, keepdims=False)
    dot = lambda part: jnp.dot(
        part.reshape(-1, depth), weight, preferred_element_type=jnp.float32
    ).reshape(part.shape[:-1] + (weight.shape[1],))
    swap = lambda value, bit: lax.ppermute(
        value, axis, [(source, source ^ (1 << bit)) for source in range(count)]
    )
    arrived = swap(dot(theirs).astype(jnp.bfloat16), 0)
    total = dot(mine)
    for bit in range(1, bits):
        mine_bit = (index >> bit) & 1
        pick = lambda value, which: lax.dynamic_index_in_dim(
            value, which, axis=bits - 1 - bit, keepdims=False
        )
        out = pick(total, 1 - mine_bit) + pick(arrived, 1 - mine_bit).astype(jnp.float32)
        total = pick(total, mine_bit) + pick(arrived, mine_bit).astype(jnp.float32)
        arrived = swap(out.astype(jnp.bfloat16), bit)
    return total + arrived.astype(jnp.float32)


def per_device(query_heads, key_heads, value_heads, segment_ids, section_input, out_weight):
    sections = lax.axis_size("pipe")
    mirrored = lax.ppermute(
        section_input, "pipe", [(source, sections - 1 - source) for source in range(sections)]
    )
    heads_out = attention(query_heads[0], key_heads[0], value_heads[0], segment_ids[0])
    width = out_weight.shape[2] // CHUNKS
    pieces = []
    for chunk in range(CHUNKS):
        columns = slice(chunk * width, (chunk + 1) * width)
        mine = scattered_sum(heads_out, out_weight[0, :, columns], "tensor")
        pieces.append((section_input[0, :, columns].astype(jnp.float32) + mine).astype(jnp.bfloat16))
    section_out = jnp.concatenate(pieces, axis=1)
    received = lax.ppermute(
        section_out[None], "pipe", [(source, source + 1) for source in range(sections - 1)]
    )
    wide = mirrored.astype(jnp.float32)
    scale = jnp.max(jnp.abs(wide), axis=2) + 1e-06
    evicted = (wide / scale[:, :, None]).astype(jnp.bfloat16)
    return (received, evicted, scale)


def solution(mesh):
    return jax.shard_map(
        per_device,
        mesh=mesh,
        in_specs=(
            P(("dp", "pipe"), None, "tensor"),
            P(("dp", "pipe"), None, "tensor"),
            P(("dp", "pipe"), None, "tensor"),
            P(("dp", "pipe"), None),
            P(("dp", "pipe"), "tensor", None),
            P(("dp", "pipe"), "tensor", None),
        ),
        out_specs=(
            P(("dp", "pipe"), "tensor", None),
            P(("dp", "pipe"), "tensor", None),
            P(("dp", "pipe"), "tensor"),
        ),
        check_vma=False,
    )
```

time: 322 us -> 171 us (0.53); the launches traced: 317 us -> 171 us
  waiting for transfers between devices: 255 us -> 96.1 us
  matrix products: 17.2 us -> 39.5 us
  between operations: 14.1 us -> 0.83 us
  other arithmetic: 10.6 us -> 19.2 us
  local copies, waits for them, and re-layouts: 9.45 us -> 6.05 us
    reduce_scatter x1 -> x0, waiting for transfers between devices: 127 us -> none  [per_device(): lax.psum_scatter(partial_value, 'tensor', scatter_dimension=0, tiled=True)]
    ppermute x5 -> x10, waiting for transfers between devices: 128 us -> 96.1 us  [the longest x1 41.2 us: per_device(): lax.ppermute(section_out[None], 'pipe', [(source, source + 1) for source...]
    dot_general x3 -> x10, matrix products: 17.2 us -> 39.5 us  [the longest x8 36.5 us: scattered_sum(): jnp.dot(part.reshape(-1, depth), weight, preferred_element_type=jnp.float32)]
    convert_element_type x3 -> x6, other arithmetic: 1.01 us -> 14.1 us  [the longest x4 6.91 us: scattered_sum(): arrived = swap(out.astype(jnp.bfloat16), bit)]
    unnamed x16 -> x20, local copies, waits for them, and re-layouts: 7.17 us -> 4.69 us
    ppermute x5 -> x10, starting transfers between devices: 10.6 us -> 8.93 us  [the longest x8 5.16 us: scattered_sum(): lax.ppermute(value, axis, [(source, source ^ 1 << bit) for source in rang...]
  transfers between devices with their start and end apart: 6 -> 10, of which waited for: 4 -> 6; matrix products, arithmetic and copies ran while one was open for 0% -> 27% of each run, Pallas kernels for 0% -> 0%
where the time goes in v1:
time: 171 us
  waiting for transfers between devices  96.1 us (56%)
  matrix products  39.5 us (23%)
  other arithmetic  19.2 us (11%)
  starting transfers between devices  8.93 us (5%)
  local copies, waits for them, and re-layouts  6.05 us (4%)
    ppermute x1, waiting for transfers between devices, per_device(): lax.ppermute(section_out[None], 'pipe', [(source, source + 1) for source...  41.2 us
    ppermute x8, waiting for transfers between devices, scattered_sum(): lax.ppermute(value, axis, [(source, source ^ 1 << bit) for source in rang...  37.5 us
    dot_general x8, matrix products, scattered_sum(): jnp.dot(part.reshape(-1, depth), weight, preferred_element_type=jnp.float32)  36.5 us
    ppermute x1, waiting for transfers between devices, per_device(): lax.ppermute(section_input, 'pipe', [(source, sections - 1 - source) for...  17.5 us
    convert_element_type x4, other arithmetic, scattered_sum(): arrived = swap(out.astype(jnp.bfloat16), bit)  6.91 us
    convert_element_type x1, other arithmetic, per_device(): (section_input[0, :, columns].astype(jnp.float32) + mine).astype(jnp.bflo...  5.35 us
    ppermute x8, starting transfers between devices, scattered_sum(): lax.ppermute(value, axis, [(source, source ^ 1 << bit) for source in rang...  5.16 us
    unnamed x20, local copies, waits for them, and re-layouts  4.69 us
  transfers between devices with their start and end apart: 10, of which 6 were waited for; matrix products, arithmetic and copies ran while one was open for 27% of the time, Pallas kernels for 0%

profile of v1, /device:TPU:16, one launch (start us, length us, event | category | flops | bytes accessed | tf_op | source)
XLA Modules:
  0.0 170.7 jit_solution(301484024284536124)
XLA Ops:
  0.7 1.6 copy.20
  2.2 1.5 copy.19
  4.2 1.3 fusion.51
  5.5 3.8 %fusion.86 = (f32[8,512]{1,0:T(8,128)S(1)}, f32[8,512,512]{1,2,0:T(8,128)S(1)}) fusion(f32[8,512,512]{1,2,0:T(8,128)S(1)} %fusion.51, pred[512,512]{0,1:T(8,128)(4,1)S(1)} %fusion.54), kind=kOutput, calls=%fused_computation.98 | output fusion | flops 12583423 | bytes 17055744 | tf_op jit(solution)/shard_map/sub | solution.py:27
  9.3 1.8 %fusion.45 = bf16[512,8,128]{2,0,1:T(8,128)(2,1)S(1)} fusion(f32[8,512,512]{1,2,0:T(8,128)S(1)} %get-tuple-element.10, f32[8,512]{1,0:T(8,128)S(1)} %get-tuple-element.9, bf16[512,8,128]{2,1,0:T(8,128)(2,1)S(1)} %bitcast.107), kind=kOutput, calls=%fused_computation.43 | convolution fusion | flops 541589504 | bytes 10502144 | tf_op jit(solution)/shard_map/hqk,khd->qhd/dot_general | solution.py:29
  11.1 0.7 copy.17
  11.8 0.7 reshape_reshape.2
  12.5 4.8 %fusion.32 = bf16[2,128,2048]{2,1,0:T(8,128)(2,1)} fusion(bf16[1,1024,8192]{2,1,0:T(8,128)(2,1)} %param.11, bf16[2,2,128,1024]{3,2,1,0:T(8,128)(2,1)S(1)} %reshape_reshape.2, s32[]{:T(128)S(6)} %select_n.42), kind=kOutput, calls=%fused_computation.37 | convolution fusion | flops 1074266112 | bytes 5767172 | tf_op jit(solution)/shard_map/dot_general | solution.py:42
  17.3 4.4 %fusion.41 = bf16[2,128,2048]{2,1,0:T(8,128)(2,1)} fusion(bf16[1,1024,8192]{2,1,0:T(8,128)(2,1)} %param.11, bf16[2,2,128,1024]{3,2,1,0:T(8,128)(2,1)S(1)} %reshape_reshape.2, s32[]{:T(128)S(6)} %select_n.42), kind=kOutput, calls=%fused_computation.40 | convolution fusion | flops 1074266112 | bytes 5767172 | tf_op jit(solution)/shard_map/dot_general | solution.py:42
  22.3 4.5 %fusion.35 = bf16[2,128,2048]{2,1,0:T(8,128)(2,1)} fusion(bf16[1,1024,8192]{2,1,0:T(8,128)(2,1)} %param.11, bf16[2,2,128,1024]{3,2,1,0:T(8,128)(2,1)S(1)} %reshape_reshape.2, s32[]{:T(128)S(6)} %select_n.42), kind=kOutput, calls=%fused_computation.38 | convolution fusion | flops 1074266112 | bytes 5767172 | tf_op jit(solution)/shard_map/dot_general | solution.py:42
  26.8 4.5 %fusion.38 = bf16[2,128,2048]{2,1,0:T(8,128)(2,1)} fusion(bf16[1,1024,8192]{2,1,0:T(8,128)(2,1)} %param.11, bf16[2,2,128,1024]{3,2,1,0:T(8,128)(2,1)S(1)} %reshape_reshape.2, s32[]{:T(128)S(6)} %select_n.42), kind=kOutput, calls=%fused_computation.39 | convolution fusion | flops 1074266112 | bytes 5767172 | tf_op jit(solution)/shard_map/dot_general | solution.py:42
  32.2 5.0 %fusion.18 = f32[2,128,2048]{2,1,0:T(8,128)} fusion(bf16[1,1024,8192]{2,1,0:T(8,128)(2,1)} %param.11, bf16[2,2,128,1024]{3,2,1,0:T(8,128)(2,1)} %copy-done.5, s32[]{:T(128)S(6)} %select_n.40), kind=kOutput, calls=%fused_computation.23 | convolution fusion | flops 1073741824 | bytes 6815748 | tf_op jit(solution)/shard_map/dot_general | solution.py:42
  37.2 4.8 %fusion.6 = f32[2,128,2048]{2,1,0:T(8,128)} fusion(bf16[1,1024,8192]{2,1,0:T(8,128)(2,1)} %param.11, bf16[2,2,128,1024]{3,2,1,0:T(8,128)(2,1)S(1)} %copy-done.6, s32[]{:T(128)S(6)} %select_n.40), kind=kOutput, calls=%fused_computation.11 | convolution fusion | flops 1073741824 | bytes 6815748 | tf_op jit(solution)/shard_map/dot_general | solution.py:42
  41.9 4.8 %fusion.14 = f32[2,128,2048]{2,1,0:T(8,128)} fusion(bf16[1,1024,8192]{2,1,0:T(8,128)(2,1)} %param.11, bf16[2,2,128,1024]{3,2,1,0:T(8,128)(2,1)S(1)} %copy-done.6, s32[]{:T(128)S(6)} %select_n.40), kind=kOutput, calls=%fused_computation.19 | convolution fusion | flops 1073741824 | bytes 6815748 | tf_op jit(solution)/shard_map/dot_general | solution.py:42
  46.7 3.7 %fusion.10 = f32[2,128,2048]{2,1,0:T(8,128)S(1)} fusion(bf16[1,1024,8192]{2,1,0:T(8,128)(2,1)} %param.11, bf16[2,2,128,1024]{3,2,1,0:T(8,128)(2,1)} %copy-done.5, s32[]{:T(128)S(6)} %select_n.40), kind=kOutput, calls=%fused_computation.15 | convolution fusion | flops 1073741824 | bytes 6815748 | tf_op jit(solution)/shard_map/dot_general | solution.py:42
  50.5 0.9 fusion.55
  51.5 1.5 collective-permute-start.1
  53.0 2.0 %fusion.58 = bf16[128,2048]{1,0:T(8,128)(2,1)} fusion(f32[2,128,2048]{2,1,0:T(8,128)S(1)} %copy-done.1, s32[]{:T(128)S(6)} %select_n.43, bf16[2,128,2048]{2,1,0:T(8,128)(2,1)} %collective-permute-done.6), kind=kLoop, calls=%fused_computation.69 | loop fusion | flops 786432 | bytes 2097156 | tf_op jit(solution)/shard_map/convert_element_type | solution.py:57
  55.0 0.6 collective-permute-start.7
  55.6 2.0 %fusion.56 = bf16[128,2048]{1,0:T(8,128)(2,1)} fusion(f32[2,128,2048]{2,1,0:T(8,128)S(1)} %copy-done.2, s32[]{:T(128)S(6)} %select_n.43, bf16[2,128,2048]{2,1,0:T(8,128)(2,1)} %collective-permute-done.2), kind=kLoop, calls=%fused_computation.67 | loop fusion | flops 786432 | bytes 2097156 | tf_op jit(solution)/shard_map/convert_element_type | solution.py:57
  57.5 1.4 collective-permute-start.3
  59.0 2.0 %fusion.57 = bf16[128,2048]{1,0:T(8,128)(2,1)} fusion(f32[2,128,2048]{2,1,0:T(8,128)S(1)} %fusion.10, s32[]{:T(128)S(6)} %select_n.43, bf16[2,128,2048]{2,1,0:T(8,128)(2,1)} %collective-permute-done.4), kind=kLoop, calls=%fused_computation.68 | loop fusion | flops 786432 | bytes 2097156 | tf_op jit(solution)/shard_map/convert_element_type | solution.py:57
  61.6 5.0 %collective-permute-done.1 = bf16[128,2048]{1,0:T(8,128)(2,1)} collective-permute-done((bf16[128,2048]{1,0:T(8,128)(2,1)}, bf16[128,2048]{1,0:T(8,128)(2,1)}, u32[]{:S(2)}, u32[]{:S(2)}) %collective-permute-start.1) | collective-permute-done | bytes 524320 | tf_op jit(solution)/shard_map/ppermute | solution.py:45
  66.6 11.2 %collective-permute-done.7 = bf16[128,2048]{1,0:T(8,128)(2,1)} collective-permute-done((bf16[128,2048]{1,0:T(8,128)(2,1)}, bf16[128,2048]{1,0:T(8,128)(2,1)}, u32[]{:S(2)}, u32[]{:S(2)}) %collective-permute-start.7) | collective-permute-done | bytes 524320 | tf_op jit(solution)/shard_map/ppermute | solution.py:45
  77.8 11.2 %collective-permute-done.3 = bf16[128,2048]{1,0:T(8,128)(2,1)} collective-permute-done((bf16[128,2048]{1,0:T(8,128)(2,1)}, bf16[128,2048]{1,0:T(8,128)(2,1)}, u32[]{:S(2)}, u32[]{:S(2)}) %collective-permute-start.3) | collective-permute-done | bytes 524320 | tf_op jit(solution)/shard_map/ppermute | solution.py:45
  89.1 10.0 %collective-permute-done.5 = bf16[128,2048]{1,0:T(8,128)(2,1)} collective-permute-done((bf16[128,2048]{1,0:T(8,128)(2,1)}, bf16[128,2048]{1,0:T(8,128)(2,1)}, u32[]{:S(2)}, u32[]{:S(2)}) %collective-permute-start.5) | collective-permute-done | bytes 524320 | tf_op jit(solution)/shard_map/ppermute | solution.py:45
  99.0 5.3 %fusion.49 = (bf16[128,2048]{1,0:T(8,128)(2,1)S(1)}, bf16[128,2048]{1,0:T(8,128)(2,1)S(1)}, bf16[128,2048]{1,0:T(8,128)(2,1)S(1)}, bf16[128,2048]{1,0:T(8,128)(2,1)S(1)}) fusion(bf16[128,2048]{1,0:T(8,128)(2,1)} %collective-permute-done.1, f32[2,128,2048]{2,1,0:T(8,128)} %fusion.18, s32[]{:T(128)S(6)} %select_n.41, ...), kind=kLoop, calls=%fused_computation.51 | loop fusion | flops 7340032 | bytes 12582916 | tf_op jit(solution)/shard_map/convert_element_type | solution.py:72
  104.6 3.3 %collective-permute-start.8 = (bf16[1,128,8192]{2,1,0:T(8,128)(2,1)S(1)}, bf16[1,128,8192]{2,1,0:T(8,128)(2,1)S(1)}, u32[]{:S(2)}, u32[]{:S(2)}) collective-permute-start(bf16[1,128,8192]{2,1,0:T(8,128)(2,1)S(1)} %maximum_bitcast_fusion), channel_id=1, source_target_pairs={{0,8},{8,16},{16,24},{1,9},{9,17},{17,25},{2,10},{10,18},{18,26},{... | collective-permute-start | bytes 6291464 | tf_op jit(solution)/shard_map/ppermute | solution.py:74
  107.9 17.5 %collective-permute-done.9 = bf16[1,128,8192]{2,1,0:T(8,128)(2,1)S(1)} collective-permute-done((bf16[1,128,8192]{2,1,0:T(8,128)(2,1)}, bf16[1,128,8192]{2,1,0:T(8,128)(2,1)S(1)}, u32[]{:S(2)}, u32[]{:S(2)}) %collective-permute-start.9) | collective-permute-done | bytes 2097184 | tf_op jit(solution)/shard_map/ppermute | solution.py:63
  126.3 1.8 %fusion.3 = bf16[1,128,8192]{2,1,0:T(8,128)(2,1)} fusion(bf16[1,128,8192]{2,1,0:T(8,128)(2,1)S(1)} %collective-permute-done.9, f32[128]{0:T(128)S(1)} %get-tuple-element.8), kind=kLoop, calls=%fused_computation.8 | loop fusion | flops 3145728 | bytes 4194816 | tf_op jit(solution)/shard_map/convert_element_type | solution.py:79
  128.1 41.2 %collective-permute-done.8 = bf16[1,128,8192]{2,1,0:T(8,128)(2,1)S(1)} collective-permute-done((bf16[1,128,8192]{2,1,0:T(8,128)(2,1)S(1)}, bf16[1,128,8192]{2,1,0:T(8,128)(2,1)S(1)}, u32[]{:S(2)}, u32[]{:S(2)}) %collective-permute-start.8) | collective-permute-done | bytes 2097184 | tf_op jit(solution)/shard_map/ppermute | solution.py:74
  169.4 1.3 copy.29
  (31 shorter events, 3.7 us)
Async XLA Ops:
  0.6 3.1 %copy-start.7 = (s32[1,512]{1,0:T(1,128)S(1)}, s32[1,512]{1,0:T(1,128)}, u32[]{:S(2)}) copy-start(s32[1,512]{1,0:T(1,128)} %param.9) | copy-start | bytes 6148
  0.6 3.3 %copy-start.4 = (bf16[1,512,1024]{2,1,0:T(8,128)(2,1)S(1)}, bf16[1,512,1024]{2,1,0:T(8,128)(2,1)}, u32[]{:S(2)}) copy-start(bf16[1,512,1024]{2,1,0:T(8,128)(2,1)} %param.8) | copy-start | bytes 3145732
  12.5 14.3 %copy-start.5 = (bf16[2,2,128,1024]{3,2,1,0:T(8,128)(2,1)}, bf16[2,2,128,1024]{3,2,1,0:T(8,128)(2,1)S(1)}, u32[]{:S(2)}) copy-start(bf16[2,2,128,1024]{3,2,1,0:T(8,128)(2,1)S(1)} %reshape_reshape.2) | copy-start | bytes 3145732
  17.3 33.2 %collective-permute-start = (bf16[2,128,2048]{2,1,0:T(8,128)(2,1)}, bf16[2,128,2048]{2,1,0:T(8,128)(2,1)S(1)}, u32[]{:S(2)}, u32[]{:S(2)}) collective-permute-start(bf16[2,128,2048]{2,1,0:T(8,128)(2,1)} %fusion.32), channel_id=1, source_target_pairs={{0,2},{2,0},{4,6},{6,4},{1,3},{3,1},{5,7},{7,5},{8,10},{10,8},{12,... | collective-permute-start | bytes 3145736 | tf_op jit(solution)/shard_map/ppermute | solution.py:45
  21.7 31.2 %collective-permute-start.6 = (bf16[2,128,2048]{2,1,0:T(8,128)(2,1)}, bf16[2,128,2048]{2,1,0:T(8,128)(2,1)}, u32[]{:S(2)}, u32[]{:S(2)}) collective-permute-start(bf16[2,128,2048]{2,1,0:T(8,128)(2,1)} %fusion.41), channel_id=1, source_target_pairs={{0,2},{2,0},{4,6},{6,4},{1,3},{3,1},{5,7},{7,5},{8,10},{10,8},{12,... | collective-permute-start | bytes 3145736 | tf_op jit(solution)/shard_map/ppermute | solution.py:45
  26.8 28.8 %collective-permute-start.2 = (bf16[2,128,2048]{2,1,0:T(8,128)(2,1)}, bf16[2,128,2048]{2,1,0:T(8,128)(2,1)}, u32[]{:S(2)}, u32[]{:S(2)}) collective-permute-start(bf16[2,128,2048]{2,1,0:T(8,128)(2,1)} %fusion.35), channel_id=1, source_target_pairs={{0,2},{2,0},{4,6},{6,4},{1,3},{3,1},{5,7},{7,5},{8,10},{10,8},{12,... | collective-permute-start | bytes 3145736 | tf_op jit(solution)/shard_map/ppermute | solution.py:45
  31.2 27.8 %collective-permute-start.4 = (bf16[2,128,2048]{2,1,0:T(8,128)(2,1)}, bf16[2,128,2048]{2,1,0:T(8,128)(2,1)}, u32[]{:S(2)}, u32[]{:S(2)}) collective-permute-start(bf16[2,128,2048]{2,1,0:T(8,128)(2,1)} %fusion.38), channel_id=1, source_target_pairs={{0,2},{2,0},{4,6},{6,4},{1,3},{3,1},{5,7},{7,5},{8,10},{10,8},{12,... | collective-permute-start | bytes 3145736 | tf_op jit(solution)/shard_map/ppermute | solution.py:45
  31.7 93.6 %collective-permute-start.9 = (bf16[1,128,8192]{2,1,0:T(8,128)(2,1)}, bf16[1,128,8192]{2,1,0:T(8,128)(2,1)S(1)}, u32[]{:S(2)}, u32[]{:S(2)}) collective-permute-start(bf16[1,128,8192]{2,1,0:T(8,128)(2,1)} %param.10), channel_id=1, source_target_pairs={{0,24},{8,16},{16,8},{24,0},{1,25},{9,17},{17,9},{25,1},{2,26},{10... | collective-permute-start | bytes 6291464 | tf_op jit(solution)/shard_map/ppermute | solution.py:63
  32.2 5.0 %copy-start.6 = (bf16[2,2,128,1024]{3,2,1,0:T(8,128)(2,1)S(1)}, bf16[2,2,128,1024]{3,2,1,0:T(8,128)(2,1)}, u32[]{:S(2)}) copy-start(bf16[2,2,128,1024]{3,2,1,0:T(8,128)(2,1)} %copy-done.5) | copy-start | bytes 3145732
  46.7 3.8 %copy-start = (f32[2,128,2048]{2,1,0:T(8,128)S(1)}, f32[2,128,2048]{2,1,0:T(8,128)}, u32[]{:S(2)}) copy-start(f32[2,128,2048]{2,1,0:T(8,128)} %fusion.18) | copy-start | bytes 6291460
  46.7 6.3 %copy-start.1 = (f32[2,128,2048]{2,1,0:T(8,128)S(1)}, f32[2,128,2048]{2,1,0:T(8,128)}, u32[]{:S(2)}) copy-start(f32[2,128,2048]{2,1,0:T(8,128)} %fusion.6) | copy-start | bytes 6291460
  50.5 10.5 %copy-start.3 = (f32[2,128,2048]{2,1,0:T(8,128)}, f32[2,128,2048]{2,1,0:T(8,128)S(1)}, u32[]{:S(2)}) copy-start(f32[2,128,2048]{2,1,0:T(8,128)S(1)} %fusion.10) | copy-start | bytes 6291460
  50.5 5.1 %copy-start.2 = (f32[2,128,2048]{2,1,0:T(8,128)S(1)}, f32[2,128,2048]{2,1,0:T(8,128)}, u32[]{:S(2)}) copy-start(f32[2,128,2048]{2,1,0:T(8,128)} %fusion.14) | copy-start | bytes 6291460
  51.5 15.1 %collective-permute-start.1 = (bf16[128,2048]{1,0:T(8,128)(2,1)}, bf16[128,2048]{1,0:T(8,128)(2,1)}, u32[]{:S(2)}, u32[]{:S(2)}) collective-permute-start(bf16[128,2048]{1,0:T(8,128)(2,1)} %fusion.55), channel_id=1, source_target_pairs={{0,4},{2,6},{4,0},{6,2},{1,5},{3,7},{5,1},{7,3},{8,12},{10,14},{12... | collective-permute-start | bytes 1572872 | tf_op jit(solution)/shard_map/ppermute | solution.py:45
  55.0 22.9 %collective-permute-start.7 = (bf16[128,2048]{1,0:T(8,128)(2,1)}, bf16[128,2048]{1,0:T(8,128)(2,1)}, u32[]{:S(2)}, u32[]{:S(2)}) collective-permute-start(bf16[128,2048]{1,0:T(8,128)(2,1)} %fusion.58), channel_id=1, source_target_pairs={{0,4},{2,6},{4,0},{6,2},{1,5},{3,7},{5,1},{7,3},{8,12},{10,14},{12... | collective-permute-start | bytes 1572872 | tf_op jit(solution)/shard_map/ppermute | solution.py:45
  57.5 31.5 %collective-permute-start.3 = (bf16[128,2048]{1,0:T(8,128)(2,1)}, bf16[128,2048]{1,0:T(8,128)(2,1)}, u32[]{:S(2)}, u32[]{:S(2)}) collective-permute-start(bf16[128,2048]{1,0:T(8,128)(2,1)} %fusion.56), channel_id=1, source_target_pairs={{0,4},{2,6},{4,0},{6,2},{1,5},{3,7},{5,1},{7,3},{8,12},{10,14},{12... | collective-permute-start | bytes 1572872 | tf_op jit(solution)/shard_map/ppermute | solution.py:45
  61.0 38.0 %collective-permute-start.5 = (bf16[128,2048]{1,0:T(8,128)(2,1)}, bf16[128,2048]{1,0:T(8,128)(2,1)}, u32[]{:S(2)}, u32[]{:S(2)}) collective-permute-start(bf16[128,2048]{1,0:T(8,128)(2,1)} %fusion.57), channel_id=1, source_target_pairs={{0,4},{2,6},{4,0},{6,2},{1,5},{3,7},{5,1},{7,3},{8,12},{10,14},{12... | collective-permute-start | bytes 1572872 | tf_op jit(solution)/shard_map/ppermute | solution.py:45
  104.6 64.8 %collective-permute-start.8 = (bf16[1,128,8192]{2,1,0:T(8,128)(2,1)S(1)}, bf16[1,128,8192]{2,1,0:T(8,128)(2,1)S(1)}, u32[]{:S(2)}, u32[]{:S(2)}) collective-permute-start(bf16[1,128,8192]{2,1,0:T(8,128)(2,1)S(1)} %maximum_bitcast_fusion), channel_id=1, source_target_pairs={{0,8},{8,16},{16,24},{1,9},{9,17},{17,25},{2,10},{10,18},{18,26},{... | collective-permute-start | bytes 6291464 | tf_op jit(solution)/shard_map/ppermute | solution.py:74

commit v2 on v1

v2 whole, which is shorter than its diff:
```python
import functools
import math

import jax
import jax.numpy as jnp
from jax import lax
from jax.experimental import pallas as pl
from jax.experimental.pallas import tpu as pltpu
from jax.sharding import PartitionSpec as P

HD = 128
CHUNKS = 4
TILE = 512
COST = pl.CostEstimate(flops=1000000, bytes_accessed=100000, transcendentals=0)
LATE = 40000000000


def attention_kernel(query_ref, key_ref, value_ref, row_ref, column_ref, out_ref):
    rows = query_ref.shape[0]
    half = rows // 2 if rows % 256 == 0 else rows
    for begin in range(0, rows, half):
        end = begin + half
        scores = lax.dot_general(
            query_ref[begin:end, :],
            key_ref[:end, :],
            (((1,), (1,)), ((), ())),
            preferred_element_type=jnp.float32,
        ) * (1.0 / math.sqrt(HD))
        query_at = lax.broadcasted_iota(jnp.int32, scores.shape, 0) + begin
        key_at = lax.broadcasted_iota(jnp.int32, scores.shape, 1)
        allowed = (column_ref[begin:end, :] == row_ref[:, :end]) & (key_at <= query_at)
        scores = jnp.where(allowed, scores, jnp.float32(-1e30))
        expons = jnp.exp(scores - jnp.max(scores, axis=1, keepdims=True))
        weights = expons * (1.0 / jnp.sum(expons, axis=1, keepdims=True))
        out_ref[begin:end, :] = jnp.dot(
            weights.astype(jnp.bfloat16), value_ref[:end, :], preferred_element_type=jnp.float32
        ).astype(jnp.bfloat16)


def attention(query, key, value, segment_ids):
    rows, width = query.shape
    head = pl.BlockSpec((rows, HD), lambda h: (0, h))
    return pl.pallas_call(
        attention_kernel,
        grid=(width // HD,),
        in_specs=[
            head,
            head,
            head,
            pl.BlockSpec((1, rows), lambda h: (0, 0)),
            pl.BlockSpec((rows, 1), lambda h: (0, 0)),
        ],
        out_specs=head,
        out_shape=jax.ShapeDtypeStruct((rows, width), jnp.bfloat16),
        compiler_params=pltpu.CompilerParams(vmem_limit_bytes=32 * 1024 * 1024),
        cost_estimate=COST,
    )(query, key, value, segment_ids.reshape(1, rows), segment_ids.reshape(rows, 1))


def projection_kernel(low_ref, heads_ref, weight_ref, theirs_ref, mine_ref):
    low = low_ref[0]
    pairs, _, rows, depth = heads_ref.shape
    theirs = heads_ref[:, 1 - low].reshape(pairs * rows, depth)
    theirs_ref[...] = (
        jnp.dot(theirs, weight_ref[...], preferred_element_type=jnp.float32)
        .astype(theirs_ref.dtype)
        .reshape(theirs_ref.shape)
    )
    mine = heads_ref[:, low].reshape(pairs * rows, depth)
    mine_ref[...] = jnp.dot(mine, weight_ref[...], preferred_element_type=jnp.float32).reshape(
        mine_ref.shape
    )


def projection(low, heads, weight, chunk, width):
    pairs, _, rows, depth = heads.shape
    tile = math.gcd(TILE, width)
    first = chunk * (width // tile)
    out = pl.BlockSpec((pairs, rows, tile), lambda i, low: (0, 0, i))
    return pl.pallas_call(
        projection_kernel,
        grid_spec=pltpu.PrefetchScalarGridSpec(
            num_scalar_prefetch=1,
            grid=(width // tile,),
            in_specs=[
                pl.BlockSpec(heads.shape, lambda i, low: (0, 0, 0, 0)),
                pl.BlockSpec((depth, tile), lambda i, low: (0, first + i)),
            ],
            out_specs=[out, out],
        ),
        out_shape=[
            jax.ShapeDtypeStruct((pairs, rows, width), jnp.bfloat16),
            jax.ShapeDtypeStruct((pairs, rows, width), jnp.float32),
        ],
        compiler_params=pltpu.CompilerParams(vmem_limit_bytes=32 * 1024 * 1024),
        cost_estimate=COST,
    )(low.reshape(1), heads, weight)


def pack_kernel(value_ref, packed_ref, scale_ref):
    wide = value_ref[...].astype(jnp.float32)
    scale = jnp.max(jnp.abs(wide), axis=1, keepdims=True) + 1e-06
    packed_ref[...] = (wide / scale).astype(packed_ref.dtype)
    scale_ref[...] = scale


def pack(value):
    rows, width = value.shape
    part = math.gcd(rows, 32)
    block = pl.BlockSpec((part, width), lambda i: (i, 0))
    return pl.pallas_call(
        pack_kernel,
        grid=(rows // part,),
        in_specs=[block],
        out_specs=[block, pl.BlockSpec((part, 1), lambda i: (i, 0))],
        out_shape=[
            jax.ShapeDtypeStruct(value.shape, value.dtype),
            jax.ShapeDtypeStruct((rows, 1), jnp.float32),
        ],
        compiler_params=pltpu.CompilerParams(vmem_limit_bytes=32 * 1024 * 1024),
        cost_estimate=pl.CostEstimate(flops=LATE, bytes_accessed=1000000, transcendentals=0),
    )(value)


def swap(value, axis, bit):
    count = lax.axis_size(axis)
    return lax.ppermute(value, axis, [(source, source ^ (1 << bit)) for source in range(count)])


def halve_kernel(own_ref, total_ref, arrived_ref, out_ref, kept_ref):
    own = own_ref[0]
    other = 1 - own
    out_ref[...] = (total_ref[:, other] + arrived_ref[:, other].astype(jnp.float32)).astype(
        out_ref.dtype
    )
    kept_ref[...] = total_ref[:, own] + arrived_ref[:, own].astype(jnp.float32)


def halve(own, total, arrived):
    groups, rows, width = total.shape
    tile = math.gcd(TILE, width)
    split = (groups // 2, 2, rows, width)
    whole = pl.BlockSpec(split[:3] + (tile,), lambda i, own: (0, 0, 0, i))
    half = pl.BlockSpec((groups // 2, rows, tile), lambda i, own: (0, 0, i))
    shape = (groups // 2, rows, width)
    return pl.pallas_call(
        halve_kernel,
        grid_spec=pltpu.PrefetchScalarGridSpec(
            num_scalar_prefetch=1,
            grid=(width // tile,),
            in_specs=[whole, whole],
            out_specs=[half, half],
        ),
        out_shape=[
            jax.ShapeDtypeStruct(shape, jnp.bfloat16),
            jax.ShapeDtypeStruct(shape, jnp.float32),
        ],
        compiler_params=pltpu.CompilerParams(vmem_limit_bytes=32 * 1024 * 1024),
        cost_estimate=COST,
    )(own.reshape(1), total.reshape(split), arrived.reshape(split))


def finish_kernel(count, *refs):
    input_ref, out_ref = refs[2 * count :]
    width = out_ref.shape[1] // count
    for chunk in range(count):
        columns = slice(chunk * width, (chunk + 1) * width)
        total = refs[chunk][...] + refs[count + chunk][...].astype(jnp.float32)
        out_ref[:, columns] = (input_ref[:, columns].astype(jnp.float32) + total).astype(
            out_ref.dtype
        )


def finish(totals, arrived, section_input):
    rows, width = section_input.shape
    count = len(totals)
    part = math.gcd(rows, 32)
    piece = pl.BlockSpec((part, width // count), lambda i: (i, 0))
    whole = pl.BlockSpec((part, width), lambda i: (i, 0))
    return pl.pallas_call(
        functools.partial(finish_kernel, count),
        grid=(rows // part,),
        in_specs=[piece] * (2 * count) + [whole],
        out_specs=whole,
        out_shape=jax.ShapeDtypeStruct(section_input.shape, section_input.dtype),
        compiler_params=pltpu.CompilerParams(vmem_limit_bytes=32 * 1024 * 1024),
        cost_estimate=COST,
    )(*totals, *arrived, section_input)


def scattered(theirs, total, axis):
    bits = lax.axis_size(axis).bit_length() - 1
    index = lax.axis_index(axis)
    arrived = swap(theirs, axis, 0)
    for bit in range(1, bits):
        out, total = halve((index >> bit) & 1, total, arrived)
        arrived = swap(out, axis, bit)
    return total[0], arrived[0]


def per_device(query_heads, key_heads, value_heads, segment_ids, section_input, out_weight):
    sections = lax.axis_size("pipe")
    tensors = lax.axis_size("tensor")
    mirrored = lax.ppermute(
        section_input, "pipe", [(source, sections - 1 - source) for source in range(sections)]
    )
    heads_out = attention(query_heads[0], key_heads[0], value_heads[0], segment_ids[0])
    rows, depth = heads_out.shape
    heads = heads_out.reshape(tensors // 2, 2, rows // tensors, depth)
    low = lax.axis_index("tensor") & 1
    width = out_weight.shape[2] // CHUNKS
    totals, arrived = [], []
    for chunk in range(CHUNKS):
        theirs, mine = projection(low, heads, out_weight[0], chunk, width)
        total, last = scattered(theirs, mine, "tensor")
        totals.append(total)
        arrived.append(last)
    section_out = finish(totals, arrived, section_input[0])
    received = lax.ppermute(
        section_out[None], "pipe", [(source, source + 1) for source in range(sections - 1)]
    )
    evicted, scale = pack(mirrored[0])
    return (received, evicted[None], scale.reshape(1, -1))


def solution(mesh):
    return jax.shard_map(
        per_device,
        mesh=mesh,
        in_specs=(
            P(("dp", "pipe"), None, "tensor"),
            P(("dp", "pipe"), None, "tensor"),
            P(("dp", "pipe"), None, "tensor"),
            P(("dp", "pipe"), None),
            P(("dp", "pipe"), "tensor", None),
            P(("dp", "pipe"), "tensor", None),
        ),
        out_specs=(
            P(("dp", "pipe"), "tensor", None),
            P(("dp", "pipe"), "tensor", None),
            P(("dp", "pipe"), "tensor"),
        ),
        check_vma=False,
    )
```

time: 171 us -> 147 us (0.86); the launches traced: 171 us -> 145 us
  matrix products: 39.5 us -> 0 us
  Pallas kernels: 0 us -> 36.9 us
  other arithmetic: 19.2 us -> 0.62 us
  waiting for transfers between devices: 96.1 us -> 79 us
  local copies, waits for them, and re-layouts: 6.05 us -> 18.4 us
    dot_general x10 -> x0, matrix products: 39.5 us -> none  [the longest x8 36.5 us: scattered_sum(): jnp.dot(part.reshape(-1, depth), weight, preferred_element_type=jnp.float32)]
    pallas_call x0 -> x11, Pallas kernels: none -> 36.9 us  [the longest x4 15.6 us: projection(): pl.pallas_call(projection_kernel, grid_spec=pltpu.PrefetchScalarGridSpec(...]
    ppermute x1, waiting for transfers between devices: 17.5 us -> 0.01 us  [per_device(): lax.ppermute(section_input, 'pipe', [(source, sections - 1 - source) for...]
    convert_element_type x6 -> x0, other arithmetic: 14.1 us -> none  [the longest x4 6.91 us: scattered_sum(): arrived = swap(out.astype(jnp.bfloat16), bit)]
    unnamed x20 -> x25, local copies, waits for them, and re-layouts: 4.69 us -> 17.6 us
    sub x1 -> x0, other arithmetic: 3.81 us -> none  [attention(): expons = jnp.exp(scores - row_max)]
  transfers between devices with their start and end apart: 10 -> 10, of which waited for: 6 -> 5; matrix products, arithmetic and copies ran while one was open for 27% -> 1% of each run, Pallas kernels for 0% -> 26%
where the time goes in v2:
time: 147 us; the launch traced here: 145 us
  waiting for transfers between devices  79 us (54%)
  Pallas kernels  36.9 us (25%)
  local copies, waits for them, and re-layouts  18.4 us (13%)
  starting transfers between devices  8.94 us (6%)
    ppermute x1, waiting for transfers between devices, per_device(): lax.ppermute(section_out[None], 'pipe', [(source, source + 1) for source...  40.9 us
    ppermute x8, waiting for transfers between devices, swap(): lax.ppermute(value, axis, [(source, source ^ 1 << bit) for source in rang...  38.1 us
    unnamed x25, local copies, waits for them, and re-layouts  17.6 us
    pallas_call x4, Pallas kernels, projection(): pl.pallas_call(projection_kernel, grid_spec=pltpu.PrefetchScalarGridSpec(...  15.6 us
    pallas_call x1, Pallas kernels, attention(): pl.pallas_call(attention_kernel, grid=(width // HD,), in_specs=[head, hea...  8.93 us
    pallas_call x4, Pallas kernels, halve(): pl.pallas_call(halve_kernel, grid_spec=pltpu.PrefetchScalarGridSpec(num_s...  7.42 us
    ppermute x8, starting transfers between devices, swap(): lax.ppermute(value, axis, [(source, source ^ 1 << bit) for source in rang...  5.36 us
    pallas_call x1, Pallas kernels, pack(): pl.pallas_call(pack_kernel, grid=(rows // part,), in_specs=[block], out_s...  4.23 us
  transfers between devices with their start and end apart: 10, of which 5 were waited for; matrix products, arithmetic and copies ran while one was open for 1% of the time, Pallas kernels for 26%

profile of v2, /device:TPU:16, one launch (start us, length us, event | category | flops | bytes accessed | tf_op | source)
XLA Modules:
  0.0 144.6 jit_solution(895258206869462929)
XLA Ops:
  1.1 0.8 copy.9.column_ref
  2.0 1.2 copy-done.8
  3.2 1.2 copy-done.9
  4.4 1.2 copy-done.10
  5.7 0.7 copy-done.11
  6.3 8.9 %shard_map.85 = bf16[512,1024]{1,0:T(8,128)(2,1)S(1)} custom-call(bf16[512,1024]{1,0:T(8,128)(2,1)S(1)} %bitcast.48, bf16[512,1024]{1,0:T(8,128)(2,1)S(1)} %bitcast.49, bf16[512,1024]{1,0:T(8,128)(2,1)S(1)} %bitcast.50, s32[1,512]{1,0:T(1,128)S(1)} %copy-done.11, s32[512,1]{1,0:T(8,128)S(1)} %copy.9.column_ref), custom_call_target="tpu_custom_call" | custom-call | flops 1000000 | bytes 100000 | tf_op jit(solution)/shard_map/pallas_call | solution.py:43
  15.3 5.8 %copy-done = bf16[1,1024,8192]{2,1,0:T(8,128)(2,1)S(1)} copy-done((bf16[1,1024,8192]{2,1,0:T(8,128)(2,1)S(1)}, bf16[1,1024,8192]{2,1,0:T(8,128)(2,1)}, u32[]{:S(2)}) %copy-start) | copy-done | bytes 16777240
  21.1 3.9 %shard_map.88 = (bf16[2,128,2048]{2,1,0:T(8,128)(2,1)}, f32[2,128,2048]{2,1,0:T(8,128)S(1)}) custom-call(s32[1]{0:T(128)} %bitcast.1.low_ref, bf16[2,2,128,1024]{3,2,1,0:T(8,128)(2,1)S(1)} %bitcast.33, bf16[1024,8192]{1,0:T(8,128)(2,1)S(1)} %bitcast.29), custom_call_target="tpu_custom_call" | custom-call | flops 1000000 | bytes 100000 | tf_op jit(solution)/shard_map/pallas_call | solution.py:80
  25.0 1.3 copy-done.6
  26.3 4.0 %shard_map.90 = (bf16[2,128,2048]{2,1,0:T(8,128)(2,1)}, f32[2,128,2048]{2,1,0:T(8,128)S(1)}) custom-call(s32[1]{0:T(128)} %bitcast.1.low_ref, bf16[2,2,128,1024]{3,2,1,0:T(8,128)(2,1)S(1)} %bitcast.34, bf16[1024,8192]{1,0:T(8,128)(2,1)S(1)} %bitcast.30), custom_call_target="tpu_custom_call" | custom-call | flops 1000000 | bytes 100000 | tf_op jit(solution)/shard_map/pallas_call | solution.py:80
  30.2 1.3 copy-done.4
  32.1 3.9 %shard_map.92 = (bf16[2,128,2048]{2,1,0:T(8,128)(2,1)}, f32[2,128,2048]{2,1,0:T(8,128)S(1)}) custom-call(s32[1]{0:T(128)} %bitcast.1.low_ref, bf16[2,2,128,1024]{3,2,1,0:T(8,128)(2,1)S(1)} %bitcast.35, bf16[1024,8192]{1,0:T(8,128)(2,1)S(1)} %bitcast.31), custom_call_target="tpu_custom_call" | custom-call | flops 1000000 | bytes 100000 | tf_op jit(solution)/shard_map/pallas_call | solution.py:80
  36.0 3.8 %shard_map.86 = (bf16[2,128,2048]{2,1,0:T(8,128)(2,1)}, f32[2,128,2048]{2,1,0:T(8,128)S(1)}) custom-call(s32[1]{0:T(128)} %bitcast.1.low_ref, bf16[2,2,128,1024]{3,2,1,0:T(8,128)(2,1)S(1)} %bitcast.36, bf16[1024,8192]{1,0:T(8,128)(2,1)S(1)} %bitcast.32), custom_call_target="tpu_custom_call" | custom-call | flops 1000000 | bytes 100000 | tf_op jit(solution)/shard_map/pallas_call | solution.py:80
  40.3 1.7 %copy-done.7 = f32[2,128,2048]{2,1,0:T(8,128)S(1)} copy-done((f32[2,128,2048]{2,1,0:T(8,128)S(1)}, f32[2,128,2048]{2,1,0:T(8,128)}, u32[]{:S(2)}) %copy-start.7) | copy-done | bytes 2097176
  42.1 2.3 %shard_map.89 = (bf16[1,128,2048]{2,1,0:T(8,128)(2,1)S(1)}, f32[1,128,2048]{2,1,0:T(8,128)S(1)}) custom-call(s32[1]{0:T(128)} %bitcast.own_ref, f32[1,2,128,2048]{3,2,1,0:T(8,128)S(1)} %bitcast.42, bf16[1,2,128,2048]{3,2,1,0:T(8,128)(2,1)} %bitcast.12.arrived_ref), custom_call_target="tpu_custom_call" | custom-call | flops 1000000 | bytes 100000 | tf_op jit(solution)/shard_map/pallas_call | solution.py:146
  44.4 1.6 %collective-permute-start.5 = (bf16[1,128,2048]{2,1,0:T(8,128)(2,1)S(1)}, bf16[1,128,2048]{2,1,0:T(8,128)(2,1)S(1)}, u32[]{:S(2)}, u32[]{:S(2)}) collective-permute-start(bf16[1,128,2048]{2,1,0:T(8,128)(2,1)S(1)} %get-tuple-element.34), channel_id=1, source_target_pairs={{0,4},{2,6},{4,0},{6,2},{1,5},{3,7},{5,1},{7,3},{8,12},{10,14},{12... | collective-permute-start | bytes 1572872 | tf_op jit(solution)/shard_map/ppermute | solution.py:127
  46.0 2.3 %shard_map.91 = (bf16[1,128,2048]{2,1,0:T(8,128)(2,1)S(1)}, f32[1,128,2048]{2,1,0:T(8,128)S(1)}) custom-call(s32[1]{0:T(128)} %bitcast.own_ref, f32[1,2,128,2048]{3,2,1,0:T(8,128)S(1)} %bitcast.41, bf16[1,2,128,2048]{3,2,1,0:T(8,128)(2,1)} %bitcast.15.arrived_ref), custom_call_target="tpu_custom_call" | custom-call | flops 1000000 | bytes 100000 | tf_op jit(solution)/shard_map/pallas_call | solution.py:146
  48.2 0.6 collective-permute-start.6
  48.8 2.3 %shard_map.93 = (bf16[1,128,2048]{2,1,0:T(8,128)(2,1)S(1)}, f32[1,128,2048]{2,1,0:T(8,128)S(1)}) custom-call(s32[1]{0:T(128)} %bitcast.own_ref, f32[1,2,128,2048]{3,2,1,0:T(8,128)S(1)} %bitcast.40, bf16[1,2,128,2048]{3,2,1,0:T(8,128)(2,1)} %bitcast.18.arrived_ref), custom_call_target="tpu_custom_call" | custom-call | flops 1000000 | bytes 100000 | tf_op jit(solution)/shard_map/pallas_call | solution.py:146
  51.1 1.6 %collective-permute-start.7 = (bf16[1,128,2048]{2,1,0:T(8,128)(2,1)S(1)}, bf16[1,128,2048]{2,1,0:T(8,128)(2,1)S(1)}, u32[]{:S(2)}, u32[]{:S(2)}) collective-permute-start(bf16[1,128,2048]{2,1,0:T(8,128)(2,1)S(1)} %get-tuple-element.36), channel_id=1, source_target_pairs={{0,4},{2,6},{4,0},{6,2},{1,5},{3,7},{5,1},{7,3},{8,12},{10,14},{12... | collective-permute-start | bytes 1572872 | tf_op jit(solution)/shard_map/ppermute | solution.py:127
  52.7 0.6 shard_map.87
  53.3 0.6 collective-permute-start.4
  53.9 5.3 %collective-permute-done.5 = bf16[1,128,2048]{2,1,0:T(8,128)(2,1)S(1)} collective-permute-done((bf16[1,128,2048]{2,1,0:T(8,128)(2,1)S(1)}, bf16[1,128,2048]{2,1,0:T(8,128)(2,1)S(1)}, u32[]{:S(2)}, u32[]{:S(2)}) %collective-permute-start.5) | collective-permute-done | bytes 524320 | tf_op jit(solution)/shard_map/ppermute | solution.py:127
  59.2 11.2 %collective-permute-done.6 = bf16[1,128,2048]{2,1,0:T(8,128)(2,1)S(1)} collective-permute-done((bf16[1,128,2048]{2,1,0:T(8,128)(2,1)S(1)}, bf16[1,128,2048]{2,1,0:T(8,128)(2,1)S(1)}, u32[]{:S(2)}, u32[]{:S(2)}) %collective-permute-start.6) | collective-permute-done | bytes 524320 | tf_op jit(solution)/shard_map/ppermute | solution.py:127
  70.4 11.2 %collective-permute-done.7 = bf16[1,128,2048]{2,1,0:T(8,128)(2,1)S(1)} collective-permute-done((bf16[1,128,2048]{2,1,0:T(8,128)(2,1)S(1)}, bf16[1,128,2048]{2,1,0:T(8,128)(2,1)S(1)}, u32[]{:S(2)}, u32[]{:S(2)}) %collective-permute-start.7) | collective-permute-done | bytes 524320 | tf_op jit(solution)/shard_map/ppermute | solution.py:127
  81.7 10.3 %collective-permute-done.4 = bf16[1,128,2048]{2,1,0:T(8,128)(2,1)S(1)} collective-permute-done((bf16[1,128,2048]{2,1,0:T(8,128)(2,1)S(1)}, bf16[1,128,2048]{2,1,0:T(8,128)(2,1)S(1)}, u32[]{:S(2)}, u32[]{:S(2)}) %collective-permute-start.4) | collective-permute-done | bytes 524320 | tf_op jit(solution)/shard_map/ppermute | solution.py:127
  92.0 0.7 shard_map.94
  92.7 3.1 %collective-permute-start.8 = (bf16[1,128,8192]{2,1,0:T(8,128)(2,1)S(1)}, bf16[1,128,8192]{2,1,0:T(8,128)(2,1)}, u32[]{:S(2)}, u32[]{:S(2)}) collective-permute-start(bf16[1,128,8192]{2,1,0:T(8,128)(2,1)S(1)} %bitcast.38), channel_id=1, source_target_pairs={{0,8},{8,16},{16,24},{1,9},{9,17},{17,25},{2,10},{10,18},{18,26},{... | collective-permute-start | bytes 6291464 | tf_op jit(solution)/shard_map/ppermute | solution.py:219
  95.8 4.2 %shard_map.95 = (bf16[128,8192]{1,0:T(8,128)(2,1)}, f32[128,1]{1,0:T(8,128)S(1)}) custom-call(bf16[128,8192]{1,0:T(8,128)(2,1)} %bitcast.26.value_ref), custom_call_target="tpu_custom_call" | custom-call | flops 40000000000 | bytes 1000000 | tf_op jit(solution)/shard_map/pallas_call | solution.py:111
  100.0 0.6 reduce
  100.6 40.9 %collective-permute-done.8 = bf16[1,128,8192]{2,1,0:T(8,128)(2,1)} collective-permute-done((bf16[1,128,8192]{2,1,0:T(8,128)(2,1)S(1)}, bf16[1,128,8192]{2,1,0:T(8,128)(2,1)}, u32[]{:S(2)}, u32[]{:S(2)}) %collective-permute-start.8) | collective-permute-done | bytes 2097184 | tf_op jit(solution)/shard_map/ppermute | solution.py:219
  141.5 3.1 %copy.11 = bf16[1,128,8192]{2,1,0:T(8,128)(2,1)} copy(bf16[1,128,8192]{2,1,0:T(8,128)(2,1)} %collective-permute-done.8) | data formatting | bytes 4194304
  (26 shorter events, 1.6 us)
Async XLA Ops:
  0.6 95.1 %collective-permute-start.9 = (bf16[1,128,8192]{2,1,0:T(8,128)(2,1)}, bf16[1,128,8192]{2,1,0:T(8,128)(2,1)}, u32[]{:S(2)}, u32[]{:S(2)}) collective-permute-start(bf16[1,128,8192]{2,1,0:T(8,128)(2,1)} %param.10), channel_id=1, source_target_pairs={{0,24},{8,16},{16,8},{24,0},{1,25},{9,17},{17,9},{25,1},{2,26},{10... | collective-permute-start | bytes 6291464 | tf_op jit(solution)/shard_map/ppermute | solution.py:204
  2.0 1.2 copy-start.8
  3.2 1.2 copy-start.9
  4.4 1.2 copy-start.10
  5.7 0.7 copy-start.11
  15.3 5.8 %copy-start = (bf16[1,1024,8192]{2,1,0:T(8,128)(2,1)S(1)}, bf16[1,1024,8192]{2,1,0:T(8,128)(2,1)}, u32[]{:S(2)}) copy-start(bf16[1,1024,8192]{2,1,0:T(8,128)(2,1)} %param.11) | copy-start | bytes 50331652
  25.0 1.3 copy-start.6
  26.3 14.0 %collective-permute-start.1 = (bf16[2,128,2048]{2,1,0:T(8,128)(2,1)}, bf16[2,128,2048]{2,1,0:T(8,128)(2,1)}, u32[]{:S(2)}, u32[]{:S(2)}) collective-permute-start(bf16[2,128,2048]{2,1,0:T(8,128)(2,1)} %get-tuple-element.25), channel_id=1, source_target_pairs={{0,2},{2,0},{4,6},{6,4},{1,3},{3,1},{5,7},{7,5},{8,10},{10,8},{12,... | collective-permute-start | bytes 3145736 | tf_op jit(solution)/shard_map/ppermute | solution.py:127
  30.2 1.3 copy-start.4
  31.6 14.4 %collective-permute-start.2 = (bf16[2,128,2048]{2,1,0:T(8,128)(2,1)}, bf16[2,128,2048]{2,1,0:T(8,128)(2,1)}, u32[]{:S(2)}, u32[]{:S(2)}) collective-permute-start(bf16[2,128,2048]{2,1,0:T(8,128)(2,1)} %get-tuple-element.28), channel_id=1, source_target_pairs={{0,2},{2,0},{4,6},{6,4},{1,3},{3,1},{5,7},{7,5},{8,10},{10,8},{12,... | collective-permute-start | bytes 3145736 | tf_op jit(solution)/shard_map/ppermute | solution.py:127
  36.0 3.9 %copy-start.2 = (f32[2,128,2048]{2,1,0:T(8,128)}, f32[2,128,2048]{2,1,0:T(8,128)S(1)}, u32[]{:S(2)}) copy-start(f32[2,128,2048]{2,1,0:T(8,128)S(1)} %get-tuple-element.30) | copy-start | bytes 6291460
  36.0 12.9 %collective-permute-start.3 = (bf16[2,128,2048]{2,1,0:T(8,128)(2,1)}, bf16[2,128,2048]{2,1,0:T(8,128)(2,1)}, u32[]{:S(2)}, u32[]{:S(2)}) collective-permute-start(bf16[2,128,2048]{2,1,0:T(8,128)(2,1)} %get-tuple-element.31), channel_id=1, source_target_pairs={{0,2},{2,0},{4,6},{6,4},{1,3},{3,1},{5,7},{7,5},{8,10},{10,8},{12,... | collective-permute-start | bytes 3145736 | tf_op jit(solution)/shard_map/ppermute | solution.py:127
  39.8 12.9 %collective-permute-start = (bf16[2,128,2048]{2,1,0:T(8,128)(2,1)}, bf16[2,128,2048]{2,1,0:T(8,128)(2,1)S(1)}, u32[]{:S(2)}, u32[]{:S(2)}) collective-permute-start(bf16[2,128,2048]{2,1,0:T(8,128)(2,1)} %get-tuple-element.22), channel_id=1, source_target_pairs={{0,2},{2,0},{4,6},{6,4},{1,3},{3,1},{5,7},{7,5},{8,10},{10,8},{12,... | collective-permute-start | bytes 3145736 | tf_op jit(solution)/shard_map/ppermute | solution.py:127
  40.3 5.6 %copy-start.5 = (f32[2,128,2048]{2,1,0:T(8,128)S(1)}, f32[2,128,2048]{2,1,0:T(8,128)}, u32[]{:S(2)}) copy-start(f32[2,128,2048]{2,1,0:T(8,128)} %copy-done.4) | copy-start | bytes 6291460
  40.3 1.7 %copy-start.7 = (f32[2,128,2048]{2,1,0:T(8,128)S(1)}, f32[2,128,2048]{2,1,0:T(8,128)}, u32[]{:S(2)}) copy-start(f32[2,128,2048]{2,1,0:T(8,128)} %copy-done.6) | copy-start | bytes 6291460
  44.3 4.5 %copy-start.3 = (f32[2,128,2048]{2,1,0:T(8,128)S(1)}, f32[2,128,2048]{2,1,0:T(8,128)}, u32[]{:S(2)}) copy-start(f32[2,128,2048]{2,1,0:T(8,128)} %copy-done.2) | copy-start | bytes 6291460
  44.4 14.9 %collective-permute-start.5 = (bf16[1,128,2048]{2,1,0:T(8,128)(2,1)S(1)}, bf16[1,128,2048]{2,1,0:T(8,128)(2,1)S(1)}, u32[]{:S(2)}, u32[]{:S(2)}) collective-permute-start(bf16[1,128,2048]{2,1,0:T(8,128)(2,1)S(1)} %get-tuple-element.34), channel_id=1, source_target_pairs={{0,4},{2,6},{4,0},{6,2},{1,5},{3,7},{5,1},{7,3},{8,12},{10,14},{12... | collective-permute-start | bytes 1572872 | tf_op jit(solution)/shard_map/ppermute | solution.py:127
  48.2 22.2 %collective-permute-start.6 = (bf16[1,128,2048]{2,1,0:T(8,128)(2,1)S(1)}, bf16[1,128,2048]{2,1,0:T(8,128)(2,1)S(1)}, u32[]{:S(2)}, u32[]{:S(2)}) collective-permute-start(bf16[1,128,2048]{2,1,0:T(8,128)(2,1)S(1)} %get-tuple-element.35), channel_id=1, source_target_pairs={{0,4},{2,6},{4,0},{6,2},{1,5},{3,7},{5,1},{7,3},{8,12},{10,14},{12... | collective-permute-start | bytes 1572872 | tf_op jit(solution)/shard_map/ppermute | solution.py:127
  51.1 40.9 %copy-start.1 = (bf16[1,128,8192]{2,1,0:T(8,128)(2,1)S(1)}, bf16[1,128,8192]{2,1,0:T(8,128)(2,1)}, u32[]{:S(2)}) copy-start(bf16[1,128,8192]{2,1,0:T(8,128)(2,1)} %param.10) | copy-start | bytes 6291460
  51.1 30.5 %collective-permute-start.7 = (bf16[1,128,2048]{2,1,0:T(8,128)(2,1)S(1)}, bf16[1,128,2048]{2,1,0:T(8,128)(2,1)S(1)}, u32[]{:S(2)}, u32[]{:S(2)}) collective-permute-start(bf16[1,128,2048]{2,1,0:T(8,128)(2,1)S(1)} %get-tuple-element.36), channel_id=1, source_target_pairs={{0,4},{2,6},{4,0},{6,2},{1,5},{3,7},{5,1},{7,3},{8,12},{10,14},{12... | collective-permute-start | bytes 1572872 | tf_op jit(solution)/shard_map/ppermute | solution.py:127
  53.3 38.7 %collective-permute-start.4 = (bf16[1,128,2048]{2,1,0:T(8,128)(2,1)S(1)}, bf16[1,128,2048]{2,1,0:T(8,128)(2,1)S(1)}, u32[]{:S(2)}, u32[]{:S(2)}) collective-permute-start(bf16[1,128,2048]{2,1,0:T(8,128)(2,1)S(1)} %get-tuple-element.33), channel_id=1, source_target_pairs={{0,4},{2,6},{4,0},{6,2},{1,5},{3,7},{5,1},{7,3},{8,12},{10,14},{12... | collective-permute-start | bytes 1572872 | tf_op jit(solution)/shard_map/ppermute | solution.py:127
  92.7 48.8 %collective-permute-start.8 = (bf16[1,128,8192]{2,1,0:T(8,128)(2,1)S(1)}, bf16[1,128,8192]{2,1,0:T(8,128)(2,1)}, u32[]{:S(2)}, u32[]{:S(2)}) collective-permute-start(bf16[1,128,8192]{2,1,0:T(8,128)(2,1)S(1)} %bitcast.38), channel_id=1, source_target_pairs={{0,8},{8,16},{16,24},{1,9},{9,17},{17,25},{2,10},{10,18},{18,26},{... | collective-permute-start | bytes 6291464 | tf_op jit(solution)/shard_map/ppermute | solution.py:219

commit v3 on v2

v3 whole, which is shorter than its diff:
```python
import functools
import math

import jax
import jax.numpy as jnp
from jax import lax
from jax.experimental import pallas as pl
from jax.experimental.pallas import tpu as pltpu
from jax.sharding import PartitionSpec as P

HD = 128
CHUNKS = 4
TILE = 512
COST = pl.CostEstimate(flops=1000000, bytes_accessed=100000, transcendentals=0)
LATE = 40000000000
VMEM = 58 * 1024 * 1024
LAST = 16


def section_kernel(owners, chunks, low_ref, query_ref, key_ref, value_ref, ids_ref, weight_ref, *refs):
    theirs_refs, mine_refs = refs[:chunks], refs[chunks : 2 * chunks]
    heads_ref, held_ref, arrived = refs[2 * chunks :]
    step = pl.program_id(0)
    tile = held_ref.shape[2]

    def fetch(at):
        columns = pl.ds(pl.multiple_of(at * tile, tile), tile)
        return pltpu.make_async_copy(weight_ref.at[:, columns], held_ref.at[at], arrived.at[at])
    rows, depth = query_ref.shape
    part = rows // owners
    half = rows // 2
    tiles = pl.num_programs(0) // chunks

    @pl.when(step == 0)
    def _():
        for at in range(held_ref.shape[0]):
            fetch(at).start()
        query_ids = ids_ref[...].astype(jnp.float32)
        key_ids = jnp.transpose(jnp.broadcast_to(query_ids, (128, rows)))[:, :1]
        for begin in range(0, rows, half):
            end = begin + half
            key_at = lax.broadcasted_iota(jnp.int32, (end, half), 0)
            query_at = lax.broadcasted_iota(jnp.int32, (end, half), 1) + begin
            allowed = (key_ids[:end] == query_ids[:, begin:end]) & (key_at <= query_at)
            bias = jnp.where(allowed, 0.0, -1e30).astype(jnp.float32)
            for head in range(depth // HD):
                lanes = slice(head * HD, (head + 1) * HD)
                scores = lax.dot_general(
                    key_ref[:end, lanes],
                    query_ref[begin:end, lanes],
                    (((1,), (1,)), ((), ())),
                    preferred_element_type=jnp.float32,
                )
                scores = scores * (math.log2(math.e) / math.sqrt(HD)) + bias
                expons = jnp.exp2(scores - jnp.max(scores, axis=0, keepdims=True))
                weights = expons * (1.0 / jnp.sum(expons, axis=0, keepdims=True))
                out = lax.dot_general(
                    value_ref[:end, lanes],
                    weights.astype(jnp.bfloat16),
                    (((0,), (0,)), ((), ())),
                    preferred_element_type=jnp.float32,
                )
                out = jnp.transpose(out).astype(jnp.bfloat16)
                for owner in range(begin // part, end // part):
                    place = jnp.where(low_ref[0] == owner % 2, half, 0) + owner // 2 * part
                    heads_ref[pl.ds(pl.multiple_of(place, part), part), lanes] = out[
                        owner * part - begin : (owner + 1) * part - begin
                    ]

    fetch(step).wait()
    product = jnp.dot(heads_ref[...], held_ref[step], preferred_element_type=jnp.float32)
    for chunk in range(chunks):

        @pl.when(step // tiles == chunk)
        def _(chunk=chunk):
            theirs, mine = theirs_refs[chunk], mine_refs[chunk]
            theirs[...] = product[:half].astype(theirs.dtype).reshape(theirs.shape)
            mine[...] = product[half:].reshape(mine.shape)


def section(owners, low, query, key, value, segment_ids, weight):
    rows, depth = query.shape
    columns = weight.shape[1]
    width = columns // CHUNKS
    tile = math.gcd(TILE, width)
    tiles = width // tile
    shape = (owners // 2, rows // owners, width)
    full = lambda array: pl.BlockSpec(array.shape, lambda i, low: (0, 0))

    def piece(chunk):
        return pl.BlockSpec(
            shape[:2] + (tile,), lambda i, low: (0, 0, jnp.clip(i - chunk * tiles, 0, tiles - 1))
        )

    ids = segment_ids.reshape(1, rows)
    out = pl.pallas_call(
        functools.partial(section_kernel, owners, CHUNKS),
        grid_spec=pltpu.PrefetchScalarGridSpec(
            num_scalar_prefetch=1,
            grid=(columns // tile,),
            in_specs=[
                full(query),
                full(key),
                full(value),
                full(ids),
                pl.BlockSpec(memory_space=pl.ANY),
            ],
            out_specs=[piece(chunk) for chunk in range(CHUNKS)] * 2,
            scratch_shapes=[
                pltpu.VMEM((rows, depth), jnp.bfloat16),
                pltpu.VMEM((columns // tile, depth, tile), jnp.bfloat16),
                pltpu.SemaphoreType.DMA((columns // tile,)),
            ],
        ),
        out_shape=[jax.ShapeDtypeStruct(shape, jnp.bfloat16)] * CHUNKS
        + [jax.ShapeDtypeStruct(shape, jnp.float32)] * CHUNKS,
        compiler_params=pltpu.CompilerParams(vmem_limit_bytes=VMEM),
        cost_estimate=COST,
    )(low.reshape(1), query, key, value, ids, weight)
    return out[:CHUNKS], out[CHUNKS:]


def pack_kernel(value_ref, packed_ref, scale_ref):
    wide = value_ref[...].astype(jnp.float32)
    scale = jnp.max(jnp.abs(wide), axis=1, keepdims=True) + 1e-06
    packed_ref[...] = (wide / scale).astype(packed_ref.dtype)
    scale_ref[...] = scale


def pack(value):
    rows, width = value.shape
    part = math.gcd(rows, 32)
    block = pl.BlockSpec((part, width), lambda i: (i, 0))
    return pl.pallas_call(
        pack_kernel,
        grid=(rows // part,),
        in_specs=[block],
        out_specs=[block, pl.BlockSpec((part, 1), lambda i: (i, 0))],
        out_shape=[
            jax.ShapeDtypeStruct(value.shape, value.dtype),
            jax.ShapeDtypeStruct((rows, 1), jnp.float32),
        ],
        compiler_params=pltpu.CompilerParams(vmem_limit_bytes=61 * 1024 * 1024),
        cost_estimate=pl.CostEstimate(flops=LATE, bytes_accessed=1000000, transcendentals=0),
    )(value)


def swap(value, axis, bit):
    count = lax.axis_size(axis)
    return lax.ppermute(value, axis, [(source, source ^ (1 << bit)) for source in range(count)])


def halve_kernel(own_ref, total_ref, arrived_ref, out_ref, kept_ref):
    own = own_ref[0]
    other = 1 - own
    out_ref[...] = (total_ref[:, other] + arrived_ref[:, other].astype(jnp.float32)).astype(
        out_ref.dtype
    )
    kept_ref[...] = total_ref[:, own] + arrived_ref[:, own].astype(jnp.float32)


def halve(own, total, arrived):
    groups, rows, width = total.shape
    tile = math.gcd(TILE, width)
    split = (groups // 2, 2, rows, width)
    whole = pl.BlockSpec(split[:3] + (tile,), lambda i, own: (0, 0, 0, i))
    half = pl.BlockSpec((groups // 2, rows, tile), lambda i, own: (0, 0, i))
    shape = (groups // 2, rows, width)
    return pl.pallas_call(
        halve_kernel,
        grid_spec=pltpu.PrefetchScalarGridSpec(
            num_scalar_prefetch=1,
            grid=(width // tile,),
            in_specs=[whole, whole],
            out_specs=[half, half],
        ),
        out_shape=[
            jax.ShapeDtypeStruct(shape, jnp.bfloat16),
            jax.ShapeDtypeStruct(shape, jnp.float32),
        ],
        compiler_params=pltpu.CompilerParams(vmem_limit_bytes=16 * 1024 * 1024),
        cost_estimate=COST,
    )(own.reshape(1), total.reshape(split), arrived.reshape(split))


def finish_kernel(count, *refs):
    input_ref, *out_refs = refs[2 * count :]
    width = input_ref.shape[1] // count

    def write(out_ref):
        for chunk in range(count):
            columns = slice(chunk * width, (chunk + 1) * width)
            total = refs[chunk][...] + refs[count + chunk][...].astype(jnp.float32)
            out_ref[:, columns] = (input_ref[:, columns].astype(jnp.float32) + total).astype(
                out_ref.dtype
            )

    is_last = pl.program_id(0) == pl.num_programs(0) - 1
    pl.when(jnp.logical_not(is_last))(lambda: write(out_refs[0]))
    pl.when(is_last)(lambda: write(out_refs[1]))


def finish(totals, arrived, section_input):
    rows, width = section_input.shape
    count = len(totals)
    part = math.gcd(rows // 2, LAST)
    piece = pl.BlockSpec((part, width // count), lambda i: (i, 0))
    whole = pl.BlockSpec((part, width), lambda i: (i, 0))
    steps = rows // part
    return pl.pallas_call(
        functools.partial(finish_kernel, count),
        grid=(steps,),
        in_specs=[piece] * (2 * count) + [whole],
        out_specs=[
            pl.BlockSpec((part, width), lambda i: (jnp.minimum(i, steps - 2), 0)),
            pl.BlockSpec((part, width), lambda i: (0, 0)),
        ],
        out_shape=[
            jax.ShapeDtypeStruct((rows - part, width), section_input.dtype),
            jax.ShapeDtypeStruct((part, width), section_input.dtype),
        ],
        compiler_params=pltpu.CompilerParams(vmem_limit_bytes=16 * 1024 * 1024),
        cost_estimate=COST,
    )(*totals, *arrived, section_input)


def place_kernel(first, part_ref, *refs):
    out_ref, sent = refs[-2:]
    rows = part_ref.shape[0]
    copy = pltpu.make_async_copy(part_ref, out_ref.at[pl.ds(first, rows)], sent)
    copy.start()
    copy.wait()


def place(part, first, rows, into=None):
    anywhere = pl.BlockSpec(memory_space=pl.ANY)
    operands = (part,) if into is None else (part, into)
    return pl.pallas_call(
        functools.partial(place_kernel, first),
        in_specs=[anywhere] * len(operands),
        out_specs=anywhere,
        out_shape=jax.ShapeDtypeStruct((rows, part.shape[1]), part.dtype),
        input_output_aliases={} if into is None else {1: 0},
        scratch_shapes=[pltpu.SemaphoreType.DMA],
        compiler_params=pltpu.CompilerParams(vmem_limit_bytes=16 * 1024 * 1024),
        cost_estimate=COST,
    )(*operands)


def scattered(theirs, total, axis):
    bits = lax.axis_size(axis).bit_length() - 1
    index = lax.axis_index(axis)
    arrived = swap(theirs, axis, 0)
    for bit in range(1, bits):
        out, total = halve((index >> bit) & 1, total, arrived)
        arrived = swap(out, axis, bit)
    return total[0], arrived[0]


def per_device(query_heads, key_heads, value_heads, segment_ids, section_input, out_weight):
    sections = lax.axis_size("pipe")
    tensors = lax.axis_size("tensor")
    mirrored = lax.ppermute(
        section_input, "pipe", [(source, sections - 1 - source) for source in range(sections)]
    )
    theirs, mine = section(
        tensors,
        lax.axis_index("tensor") & 1,
        query_heads[0],
        key_heads[0],
        value_heads[0],
        segment_ids[0],
        out_weight[0],
    )
    pairs = [scattered(*parts, "tensor") for parts in zip(theirs, mine)]
    totals, arrived = zip(*pairs)
    onward = [
        lax.ppermute(part, "pipe", [(source, source + 1) for source in range(sections - 1)])
        for part in finish(totals, arrived, section_input[0])
    ]
    received = place(onward[0], 0, section_input.shape[1])
    received = place(onward[1], onward[0].shape[0], section_input.shape[1], received)[None]
    evicted, scale = pack(mirrored[0])
    return (received, evicted[None], scale.reshape(1, -1))


def solution(mesh):
    return jax.shard_map(
        per_device,
        mesh=mesh,
        in_specs=(
            P(("dp", "pipe"), None, "tensor"),
            P(("dp", "pipe"), None, "tensor"),
            P(("dp", "pipe"), None, "tensor"),
            P(("dp", "pipe"), None),
            P(("dp", "pipe"), "tensor", None),
            P(("dp", "pipe"), "tensor", None),
        ),
        out_specs=(
            P(("dp", "pipe"), "tensor", None),
            P(("dp", "pipe"), "tensor", None),
            P(("dp", "pipe"), "tensor"),
        ),
        check_vma=False,
    )
```

time: 147 us -> 139 us (0.946); the launches traced: 145 us -> 139 us
  local copies, waits for them, and re-layouts: 18.4 us -> 1.61 us
  Pallas kernels: 36.9 us -> 42.3 us
  waiting for transfers between devices: 79 us -> 81.7 us
  starting transfers between devices: 8.94 us -> 11 us
    unnamed x25 -> x10, local copies, waits for them, and re-layouts: 17.6 us -> 1.61 us
    pallas_call x6 -> x4, Pallas kernels: 25.2 us -> 30.7 us  [the longest x1 25.5 us: section(): pl.pallas_call(functools.partial(section_kernel, owners, CHUNKS), grid_sp...]
    ppermute x1, waiting for transfers between devices: 0.01 us -> 4.77 us  [per_device(): lax.ppermute(section_input, 'pipe', [(source, sections - 1 - source) for...]
    ppermute x1 -> x2, waiting for transfers between devices: 40.9 us -> 36.8 us  [per_device(): lax.ppermute(part, 'pipe', [(source, source + 1) for source in range(sect...]
    ppermute x8, waiting for transfers between devices: 38.1 us -> 40.2 us  [swap(): lax.ppermute(value, axis, [(source, source ^ 1 << bit) for source in rang...]
    ppermute x1 -> x2, starting transfers between devices: 3.07 us -> 5.08 us  [per_device(): lax.ppermute(part, 'pipe', [(source, source + 1) for source in range(sect...]
  transfers between devices with their start and end apart: 10 -> 11, of which waited for: 5 -> 8; matrix products, arithmetic and copies ran while one was open for 1% -> 1% of each run, Pallas kernels for 26% -> 30%
where the time goes in v3:
time: 139 us
  waiting for transfers between devices  81.7 us (59%)
  Pallas kernels  42.3 us (30%)
  starting transfers between devices  11 us (8%)
  local copies, waits for them, and re-layouts  1.61 us (1%)
  other arithmetic  1.46 us (1%)
    ppermute x8, waiting for transfers between devices, swap(): lax.ppermute(value, axis, [(source, source ^ 1 << bit) for source in rang...  40.2 us
    ppermute x2, waiting for transfers between devices, per_device(): lax.ppermute(part, 'pipe', [(source, source + 1) for source in range(sect...  36.8 us
    pallas_call x1, Pallas kernels, section(): pl.pallas_call(functools.partial(section_kernel, owners, CHUNKS), grid_sp...  25.5 us
    pallas_call x4, Pallas kernels, halve(): pl.pallas_call(halve_kernel, grid_spec=pltpu.PrefetchScalarGridSpec(num_s...  7.42 us
    ppermute x8, starting transfers between devices, swap(): lax.ppermute(value, axis, [(source, source ^ 1 << bit) for source in rang...  5.42 us
    ppermute x2, starting transfers between devices, per_device(): lax.ppermute(part, 'pipe', [(source, source + 1) for source in range(sect...  5.08 us
    ppermute x1, waiting for transfers between devices, per_device(): lax.ppermute(section_input, 'pipe', [(source, sections - 1 - source) for...  4.77 us
    pallas_call x1, Pallas kernels, pack(): pl.pallas_call(pack_kernel, grid=(rows // part,), in_specs=[block], out_s...  4.22 us
  transfers between devices with their start and end apart: 11, of which 8 were waited for; matrix products, arithmetic and copies ran while one was open for 1% of the time, Pallas kernels for 30%

profile of v3, /device:TPU:16, one launch (start us, length us, event | category | flops | bytes accessed | tf_op | source)
XLA Modules:
  0.0 138.9 jit_solution(1193926262495352588)
XLA Ops:
  0.6 0.5 collective-permute-start.10
  1.1 25.5 %shard_map.85 = (bf16[2,128,2048]{2,1,0:T(8,128)(2,1)}, bf16[2,128,2048]{2,1,0:T(8,128)(2,1)}, bf16[2,128,2048]{2,1,0:T(8,128)(2,1)}, bf16[2,128,2048]{2,1,0:T(8...) custom-call(s32[1]{0:T(128)} %bitcast.1.low_ref, ...), custom_call_target="tpu_custom_call" | custom-call | flops 1000000 | bytes 100000 | tf_op jit(solution)/shard_map/pallas_call | solution.py:96
  26.6 0.1 collective-permute-start.3
  26.7 0.5 collective-permute-start.2
  27.2 0.1 collective-permute-start.1
  27.3 0.4 collective-permute-start
  27.7 2.0 %collective-permute-done.3 = bf16[2,128,2048]{2,1,0:T(8,128)(2,1)} collective-permute-done((bf16[2,128,2048]{2,1,0:T(8,128)(2,1)}, bf16[2,128,2048]{2,1,0:T(8,128)(2,1)}, u32[]{:S(2)}, u32[]{:S(2)}) %collective-permute-start.3) | collective-permute-done | bytes 1048608 | tf_op jit(solution)/shard_map/ppermute | solution.py:150
  29.7 1.6 %copy-done.3 = f32[2,128,2048]{2,1,0:T(8,128)S(1)} copy-done((f32[2,128,2048]{2,1,0:T(8,128)S(1)}, f32[2,128,2048]{2,1,0:T(8,128)}, u32[]{:S(2)}) %copy-start.3) | copy-done | bytes 2097176
  31.3 2.3 %shard_map.89 = (bf16[1,128,2048]{2,1,0:T(8,128)(2,1)S(1)}, f32[1,128,2048]{2,1,0:T(8,128)S(1)}) custom-call(s32[1]{0:T(128)} %bitcast.own_ref, f32[1,2,128,2048]{3,2,1,0:T(8,128)S(1)} %bitcast.30, bf16[1,2,128,2048]{3,2,1,0:T(8,128)(2,1)} %bitcast.16.arrived_ref), custom_call_target="tpu_custom_call" | custom-call | flops 1000000 | bytes 100000 | tf_op jit(solution)/shard_map/pallas_call | solution.py:169
  33.6 0.0 copy-start.1
  33.6 1.6 %collective-permute-start.7 = (bf16[1,128,2048]{2,1,0:T(8,128)(2,1)S(1)}, bf16[1,128,2048]{2,1,0:T(8,128)(2,1)S(1)}, u32[]{:S(2)}, u32[]{:S(2)}) collective-permute-start(bf16[1,128,2048]{2,1,0:T(8,128)(2,1)S(1)} %get-tuple-element.38), channel_id=1, source_target_pairs={{0,4},{2,6},{4,0},{6,2},{1,5},{3,7},{5,1},{7,3},{8,12},{10,14},{12... | collective-permute-start | bytes 1572872 | tf_op jit(solution)/shard_map/ppermute | solution.py:150
  35.2 2.3 %shard_map.88 = (bf16[1,128,2048]{2,1,0:T(8,128)(2,1)S(1)}, f32[1,128,2048]{2,1,0:T(8,128)S(1)}) custom-call(s32[1]{0:T(128)} %bitcast.own_ref, f32[1,2,128,2048]{3,2,1,0:T(8,128)S(1)} %bitcast.29, bf16[1,2,128,2048]{3,2,1,0:T(8,128)(2,1)} %bitcast.13.arrived_ref), custom_call_target="tpu_custom_call" | custom-call | flops 1000000 | bytes 100000 | tf_op jit(solution)/shard_map/pallas_call | solution.py:169
  37.5 0.0 copy-start
  37.5 0.6 collective-permute-start.6
  38.1 2.3 %shard_map.87 = (bf16[1,128,2048]{2,1,0:T(8,128)(2,1)S(1)}, f32[1,128,2048]{2,1,0:T(8,128)S(1)}) custom-call(s32[1]{0:T(128)} %bitcast.own_ref, f32[1,2,128,2048]{3,2,1,0:T(8,128)S(1)} %bitcast.28, bf16[1,2,128,2048]{3,2,1,0:T(8,128)(2,1)} %bitcast.10.arrived_ref), custom_call_target="tpu_custom_call" | custom-call | flops 1000000 | bytes 100000 | tf_op jit(solution)/shard_map/pallas_call | solution.py:169
  40.4 1.6 %collective-permute-start.5 = (bf16[1,128,2048]{2,1,0:T(8,128)(2,1)S(1)}, bf16[1,128,2048]{2,1,0:T(8,128)(2,1)S(1)}, u32[]{:S(2)}, u32[]{:S(2)}) collective-permute-start(bf16[1,128,2048]{2,1,0:T(8,128)(2,1)S(1)} %get-tuple-element.36), channel_id=1, source_target_pairs={{0,4},{2,6},{4,0},{6,2},{1,5},{3,7},{5,1},{7,3},{8,12},{10,14},{12... | collective-permute-start | bytes 1572872 | tf_op jit(solution)/shard_map/ppermute | solution.py:150
  41.9 0.6 shard_map.86
  42.5 0.6 collective-permute-start.4
  43.1 5.3 %collective-permute-done.7 = bf16[1,128,2048]{2,1,0:T(8,128)(2,1)S(1)} collective-permute-done((bf16[1,128,2048]{2,1,0:T(8,128)(2,1)S(1)}, bf16[1,128,2048]{2,1,0:T(8,128)(2,1)S(1)}, u32[]{:S(2)}, u32[]{:S(2)}) %collective-permute-start.7) | collective-permute-done | bytes 524320 | tf_op jit(solution)/shard_map/ppermute | solution.py:150
  48.4 11.2 %collective-permute-done.6 = bf16[1,128,2048]{2,1,0:T(8,128)(2,1)S(1)} collective-permute-done((bf16[1,128,2048]{2,1,0:T(8,128)(2,1)S(1)}, bf16[1,128,2048]{2,1,0:T(8,128)(2,1)S(1)}, u32[]{:S(2)}, u32[]{:S(2)}) %collective-permute-start.6) | collective-permute-done | bytes 524320 | tf_op jit(solution)/shard_map/ppermute | solution.py:150
  59.7 11.2 %collective-permute-done.5 = bf16[1,128,2048]{2,1,0:T(8,128)(2,1)S(1)} collective-permute-done((bf16[1,128,2048]{2,1,0:T(8,128)(2,1)S(1)}, bf16[1,128,2048]{2,1,0:T(8,128)(2,1)S(1)}, u32[]{:S(2)}, u32[]{:S(2)}) %collective-permute-start.5) | collective-permute-done | bytes 524320 | tf_op jit(solution)/shard_map/ppermute | solution.py:150
  70.9 10.4 %collective-permute-done.4 = bf16[1,128,2048]{2,1,0:T(8,128)(2,1)S(1)} collective-permute-done((bf16[1,128,2048]{2,1,0:T(8,128)(2,1)S(1)}, bf16[1,128,2048]{2,1,0:T(8,128)(2,1)S(1)}, u32[]{:S(2)}, u32[]{:S(2)}) %collective-permute-start.4) | collective-permute-done | bytes 524320 | tf_op jit(solution)/shard_map/ppermute | solution.py:150
  81.3 3.3 %shard_map.90 = (bf16[112,8192]{1,0:T(8,128)(2,1)}, bf16[16,8192]{1,0:T(8,128)(2,1)S(1)}) custom-call(f32[128,2048]{1,0:T(8,128)S(1)} %bitcast.36, f32[128,2048]{1,0:T(8,128)S(1)} %bitcast.35, f32[128,2048]{1,0:T(8,128)S(1)} %bitcast.34, f32[128,2048]{1,0:T(8,128)S(1)} %bitcast.33, bf16[128,2048]{1,0:T(8,128)(2,1)S(1)} %bitcast.40, ...), custom_call_target="tpu_custom_call" | custom-call | flops 1000000 | bytes 100000 | tf_op jit(solution)/shard_map/pallas_call | solution.py:210
  84.6 3.2 %collective-permute-start.9 = (bf16[112,8192]{1,0:T(8,128)(2,1)}, bf16[112,8192]{1,0:T(8,128)(2,1)S(1)}, u32[]{:S(2)}, u32[]{:S(2)}) collective-permute-start(bf16[112,8192]{1,0:T(8,128)(2,1)} %get-tuple-element.40), channel_id=1, source_target_pairs={{0,8},{8,16},{16,24},{1,9},{9,17},{17,25},{2,10},{10,18},{18,26},{... | collective-permute-start | bytes 5505032 | tf_op jit(solution)/shard_map/ppermute | solution.py:278
  87.8 1.9 %collective-permute-start.8 = (bf16[16,8192]{1,0:T(8,128)(2,1)S(1)}, bf16[16,8192]{1,0:T(8,128)(2,1)S(1)}, u32[]{:S(2)}, u32[]{:S(2)}) collective-permute-start(bf16[16,8192]{1,0:T(8,128)(2,1)S(1)} %get-tuple-element.39), channel_id=1, source_target_pairs={{0,8},{8,16},{16,24},{1,9},{9,17},{17,25},{2,10},{10,18},{18,26},{... | collective-permute-start | bytes 786440 | tf_op jit(solution)/shard_map/ppermute | solution.py:278
  89.7 4.8 %collective-permute-done.10 = bf16[1,128,8192]{2,1,0:T(8,128)(2,1)} collective-permute-done((bf16[1,128,8192]{2,1,0:T(8,128)(2,1)}, bf16[1,128,8192]{2,1,0:T(8,128)(2,1)}, u32[]{:S(2)}, u32[]{:S(2)}) %collective-permute-start.10) | collective-permute-done | bytes 2097184 | tf_op jit(solution)/shard_map/ppermute | solution.py:263
  94.5 4.2 %shard_map.93 = (bf16[128,8192]{1,0:T(8,128)(2,1)}, f32[128,1]{1,0:T(8,128)}) custom-call(bf16[128,8192]{1,0:T(8,128)(2,1)} %bitcast.24.value_ref), custom_call_target="tpu_custom_call" | custom-call | flops 40000000000 | bytes 1000000 | tf_op jit(solution)/shard_map/pallas_call | solution.py:134
  98.7 1.5 %reduce = f32[128]{0:T(128)} reduce(f32[128,1]{1,0:T(8,128)} %get-tuple-element.42, f32[]{:T(128)} %constant.14), dimensions={1}, to_apply=%get-tuple-element.42.reduce_sub_computation | reduce | bytes 1028 | tf_op jit(solution)/shard_map/pallas_call | solution.py:134
  100.2 33.5 %collective-permute-done.9.part_ref = bf16[112,8192]{1,0:T(8,128)(2,1)S(1)} collective-permute-done((bf16[112,8192]{1,0:T(8,128)(2,1)}, bf16[112,8192]{1,0:T(8,128)(2,1)S(1)}, u32[]{:S(2)}, u32[]{:S(2)}) %collective-permute-start.9) | collective-permute-done | bytes 1835040 | tf_op jit(solution)/shard_map/ppermute | solution.py:278
  133.7 1.2 shard_map.91.refs_0_
  134.9 3.2 %collective-permute-done.8.part_ref = bf16[16,8192]{1,0:T(8,128)(2,1)S(1)} collective-permute-done((bf16[16,8192]{1,0:T(8,128)(2,1)S(1)}, bf16[16,8192]{1,0:T(8,128)(2,1)S(1)}, u32[]{:S(2)}, u32[]{:S(2)}) %collective-permute-start.8) | collective-permute-done | bytes 262176 | tf_op jit(solution)/shard_map/ppermute | solution.py:278
  138.2 0.7 shard_map.92
  (10 shorter events, 0.0 us)
Async XLA Ops:
  0.6 93.8 %collective-permute-start.10 = (bf16[1,128,8192]{2,1,0:T(8,128)(2,1)}, bf16[1,128,8192]{2,1,0:T(8,128)(2,1)}, u32[]{:S(2)}, u32[]{:S(2)}) collective-permute-start(bf16[1,128,8192]{2,1,0:T(8,128)(2,1)} %param.10), channel_id=1, source_target_pairs={{0,24},{8,16},{16,8},{24,0},{1,25},{9,17},{17,9},{25,1},{2,26},{10... | collective-permute-start | bytes 6291464 | tf_op jit(solution)/shard_map/ppermute | solution.py:263
  26.6 8.6 %copy-start.2 = (f32[2,128,2048]{2,1,0:T(8,128)S(1)}, f32[2,128,2048]{2,1,0:T(8,128)}, u32[]{:S(2)}) copy-start(f32[2,128,2048]{2,1,0:T(8,128)} %get-tuple-element.29) | copy-start | bytes 6291460
  26.6 3.1 %collective-permute-start.3 = (bf16[2,128,2048]{2,1,0:T(8,128)(2,1)}, bf16[2,128,2048]{2,1,0:T(8,128)(2,1)}, u32[]{:S(2)}, u32[]{:S(2)}) collective-permute-start(bf16[2,128,2048]{2,1,0:T(8,128)(2,1)} %get-tuple-element.33), channel_id=1, source_target_pairs={{0,2},{2,0},{4,6},{6,4},{1,3},{3,1},{5,7},{7,5},{8,10},{10,8},{12,... | collective-permute-start | bytes 3145736 | tf_op jit(solution)/shard_map/ppermute | solution.py:150
  26.7 8.5 %collective-permute-start.2 = (bf16[2,128,2048]{2,1,0:T(8,128)(2,1)}, bf16[2,128,2048]{2,1,0:T(8,128)(2,1)}, u32[]{:S(2)}, u32[]{:S(2)}) collective-permute-start(bf16[2,128,2048]{2,1,0:T(8,128)(2,1)} %get-tuple-element.30), channel_id=1, source_target_pairs={{0,2},{2,0},{4,6},{6,4},{1,3},{3,1},{5,7},{7,5},{8,10},{10,8},{12,... | collective-permute-start | bytes 3145736 | tf_op jit(solution)/shard_map/ppermute | solution.py:150
  27.2 10.9 %collective-permute-start.1 = (bf16[2,128,2048]{2,1,0:T(8,128)(2,1)}, bf16[2,128,2048]{2,1,0:T(8,128)(2,1)}, u32[]{:S(2)}, u32[]{:S(2)}) collective-permute-start(bf16[2,128,2048]{2,1,0:T(8,128)(2,1)} %get-tuple-element.27), channel_id=1, source_target_pairs={{0,2},{2,0},{4,6},{6,4},{1,3},{3,1},{5,7},{7,5},{8,10},{10,8},{12,... | collective-permute-start | bytes 3145736 | tf_op jit(solution)/shard_map/ppermute | solution.py:150
  27.3 14.7 %collective-permute-start = (bf16[2,128,2048]{2,1,0:T(8,128)(2,1)}, bf16[2,128,2048]{2,1,0:T(8,128)(2,1)S(1)}, u32[]{:S(2)}, u32[]{:S(2)}) collective-permute-start(bf16[2,128,2048]{2,1,0:T(8,128)(2,1)} %get-tuple-element.24), channel_id=1, source_target_pairs={{0,2},{2,0},{4,6},{6,4},{1,3},{3,1},{5,7},{7,5},{8,10},{10,8},{12,... | collective-permute-start | bytes 3145736 | tf_op jit(solution)/shard_map/ppermute | solution.py:150
  29.7 1.6 %copy-start.3 = (f32[2,128,2048]{2,1,0:T(8,128)S(1)}, f32[2,128,2048]{2,1,0:T(8,128)}, u32[]{:S(2)}) copy-start(f32[2,128,2048]{2,1,0:T(8,128)} %get-tuple-element.32) | copy-start | bytes 6291460
  33.6 4.5 %copy-start.1 = (f32[2,128,2048]{2,1,0:T(8,128)S(1)}, f32[2,128,2048]{2,1,0:T(8,128)}, u32[]{:S(2)}) copy-start(f32[2,128,2048]{2,1,0:T(8,128)} %get-tuple-element.26) | copy-start | bytes 6291460
  33.6 14.8 %collective-permute-start.7 = (bf16[1,128,2048]{2,1,0:T(8,128)(2,1)S(1)}, bf16[1,128,2048]{2,1,0:T(8,128)(2,1)S(1)}, u32[]{:S(2)}, u32[]{:S(2)}) collective-permute-start(bf16[1,128,2048]{2,1,0:T(8,128)(2,1)S(1)} %get-tuple-element.38), channel_id=1, source_target_pairs={{0,4},{2,6},{4,0},{6,2},{1,5},{3,7},{5,1},{7,3},{8,12},{10,14},{12... | collective-permute-start | bytes 1572872 | tf_op jit(solution)/shard_map/ppermute | solution.py:150
  37.5 4.5 %copy-start = (f32[2,128,2048]{2,1,0:T(8,128)S(1)}, f32[2,128,2048]{2,1,0:T(8,128)}, u32[]{:S(2)}) copy-start(f32[2,128,2048]{2,1,0:T(8,128)} %get-tuple-element.23) | copy-start | bytes 6291460
  37.5 22.2 %collective-permute-start.6 = (bf16[1,128,2048]{2,1,0:T(8,128)(2,1)S(1)}, bf16[1,128,2048]{2,1,0:T(8,128)(2,1)S(1)}, u32[]{:S(2)}, u32[]{:S(2)}) collective-permute-start(bf16[1,128,2048]{2,1,0:T(8,128)(2,1)S(1)} %get-tuple-element.37), channel_id=1, source_target_pairs={{0,4},{2,6},{4,0},{6,2},{1,5},{3,7},{5,1},{7,3},{8,12},{10,14},{12... | collective-permute-start | bytes 1572872 | tf_op jit(solution)/shard_map/ppermute | solution.py:150
  40.4 41.0 %copy-start.4 = (bf16[1,128,8192]{2,1,0:T(8,128)(2,1)S(1)}, bf16[1,128,8192]{2,1,0:T(8,128)(2,1)}, u32[]{:S(2)}) copy-start(bf16[1,128,8192]{2,1,0:T(8,128)(2,1)} %param.10) | copy-start | bytes 6291460
  40.4 30.5 %collective-permute-start.5 = (bf16[1,128,2048]{2,1,0:T(8,128)(2,1)S(1)}, bf16[1,128,2048]{2,1,0:T(8,128)(2,1)S(1)}, u32[]{:S(2)}, u32[]{:S(2)}) collective-permute-start(bf16[1,128,2048]{2,1,0:T(8,128)(2,1)S(1)} %get-tuple-element.36), channel_id=1, source_target_pairs={{0,4},{2,6},{4,0},{6,2},{1,5},{3,7},{5,1},{7,3},{8,12},{10,14},{12... | collective-permute-start | bytes 1572872 | tf_op jit(solution)/shard_map/ppermute | solution.py:150
  42.5 38.8 %collective-permute-start.4 = (bf16[1,128,2048]{2,1,0:T(8,128)(2,1)S(1)}, bf16[1,128,2048]{2,1,0:T(8,128)(2,1)S(1)}, u32[]{:S(2)}, u32[]{:S(2)}) collective-permute-start(bf16[1,128,2048]{2,1,0:T(8,128)(2,1)S(1)} %get-tuple-element.35), channel_id=1, source_target_pairs={{0,4},{2,6},{4,0},{6,2},{1,5},{3,7},{5,1},{7,3},{8,12},{10,14},{12... | collective-permute-start | bytes 1572872 | tf_op jit(solution)/shard_map/ppermute | solution.py:150
  84.6 49.1 %collective-permute-start.9 = (bf16[112,8192]{1,0:T(8,128)(2,1)}, bf16[112,8192]{1,0:T(8,128)(2,1)S(1)}, u32[]{:S(2)}, u32[]{:S(2)}) collective-permute-start(bf16[112,8192]{1,0:T(8,128)(2,1)} %get-tuple-element.40), channel_id=1, source_target_pairs={{0,8},{8,16},{16,24},{1,9},{9,17},{17,25},{2,10},{10,18},{18,26},{... | collective-permute-start | bytes 5505032 | tf_op jit(solution)/shard_map/ppermute | solution.py:278
  87.8 50.4 %collective-permute-start.8 = (bf16[16,8192]{1,0:T(8,128)(2,1)S(1)}, bf16[16,8192]{1,0:T(8,128)(2,1)S(1)}, u32[]{:S(2)}, u32[]{:S(2)}) collective-permute-start(bf16[16,8192]{1,0:T(8,128)(2,1)S(1)} %get-tuple-element.39), channel_id=1, source_target_pairs={{0,8},{8,16},{16,24},{1,9},{9,17},{17,25},{2,10},{10,18},{18,26},{... | collective-permute-start | bytes 786440 | tf_op jit(solution)/shard_map/ppermute | solution.py:278

commit v4 on v3

--- a/solution.py
+++ b/solution.py
@@ -43,8 +43,9 @@
             query_at = lax.broadcasted_iota(jnp.int32, (end, half), 1) + begin
             allowed = (key_ids[:end] == query_ids[:, begin:end]) & (key_at <= query_at)
             bias = jnp.where(allowed, 0.0, -1e30).astype(jnp.float32)
-            for head in range(depth // HD):
-                lanes = slice(head * HD, (head + 1) * HD)
+
+            def one_head(head, carry, begin=begin, end=end, bias=bias):
+                lanes = pl.ds(pl.multiple_of(head * HD, HD), HD)
                 scores = lax.dot_general(
                     key_ref[:end, lanes],
                     query_ref[begin:end, lanes],
@@ -66,6 +67,9 @@
                     heads_ref[pl.ds(pl.multiple_of(place, part), part), lanes] = out[
                         owner * part - begin : (owner + 1) * part - begin
                     ]
+                return carry
+
+            lax.fori_loop(0, depth // HD, one_head, 0)
 
     fetch(step).wait()
     product = jnp.dot(heads_ref[...], held_ref[step], preferred_element_type=jnp.float32)
@@ -224,27 +228,23 @@
     )(*totals, *arrived, section_input)
 
 
-def place_kernel(first, part_ref, *refs):
-    out_ref, sent = refs[-2:]
-    rows = part_ref.shape[0]
-    copy = pltpu.make_async_copy(part_ref, out_ref.at[pl.ds(first, rows)], sent)
+def place_kernel(part_ref, out_ref, sent):
+    copy = pltpu.make_async_copy(part_ref, out_ref.at[: part_ref.shape[0]], sent)
     copy.start()
     copy.wait()
 
 
-def place(part, first, rows, into=None):
+def place(part, rows):
     anywhere = pl.BlockSpec(memory_space=pl.ANY)
-    operands = (part,) if into is None else (part, into)
     return pl.pallas_call(
-        functools.partial(place_kernel, first),
-        in_specs=[anywhere] * len(operands),
+        place_kernel,
+        in_specs=[anywhere],
         out_specs=anywhere,
         out_shape=jax.ShapeDtypeStruct((rows, part.shape[1]), part.dtype),
-        input_output_aliases={} if into is None else {1: 0},
         scratch_shapes=[pltpu.SemaphoreType.DMA],
         compiler_params=pltpu.CompilerParams(vmem_limit_bytes=16 * 1024 * 1024),
         cost_estimate=COST,
-    )(*operands)
+    )(part)
 
 
 def scattered(theirs, total, axis):
@@ -278,8 +278,8 @@
         lax.ppermute(part, "pipe", [(source, source + 1) for source in range(sections - 1)])
         for part in finish(totals, arrived, section_input[0])
     ]
-    received = place(onward[0], 0, section_input.shape[1])
-    received = place(onward[1], onward[0].shape[0], section_input.shape[1], received)[None]
+    received = place(onward[0], section_input.shape[1])
+    received = lax.dynamic_update_slice(received, onward[1], (onward[0].shape[0], 0))[None]
     evicted, scale = pack(mirrored[0])
     return (received, evicted[None], scale.reshape(1, -1))
 

time: 139 us -> 139 us (level)
  waiting for transfers between devices: 81.7 us -> 79.2 us
  Pallas kernels: 42.3 us -> 44.1 us
    pallas_call x1, Pallas kernels: 25.5 us -> 27.9 us  [section(): pl.pallas_call(functools.partial(section_kernel, owners, CHUNKS), grid_sp...]
    ppermute x1, waiting for transfers between devices: 4.77 us -> 2.28 us  [per_device(): lax.ppermute(section_input, 'pipe', [(source, sections - 1 - source) for...]
  transfers between devices with their start and end apart: 11 -> 11, of which waited for: 8 -> 8; matrix products, arithmetic and copies ran while one was open for 1% -> 1% of each run, Pallas kernels for 30% -> 32%
where the time goes in v4:
time: 139 us
  waiting for transfers between devices  79.2 us (57%)
  Pallas kernels  44.1 us (32%)
  starting transfers between devices  11 us (8%)
  local copies, waits for them, and re-layouts  2.33 us (2%)
  other arithmetic  1.46 us (1%)
    ppermute x8, waiting for transfers between devices, swap(): lax.ppermute(value, axis, [(source, source ^ 1 << bit) for source in rang...  40.2 us
    ppermute x2, waiting for transfers between devices, per_device(): lax.ppermute(part, 'pipe', [(source, source + 1) for source in range(sect...  36.8 us
    pallas_call x1, Pallas kernels, section(): pl.pallas_call(functools.partial(section_kernel, owners, CHUNKS), grid_sp...  27.9 us
    pallas_call x4, Pallas kernels, halve(): pl.pallas_call(halve_kernel, grid_spec=pltpu.PrefetchScalarGridSpec(num_s...  7.42 us
    ppermute x8, starting transfers between devices, swap(): lax.ppermute(value, axis, [(source, source ^ 1 << bit) for source in rang...  5.42 us
    ppermute x2, starting transfers between devices, per_device(): lax.ppermute(part, 'pipe', [(source, source + 1) for source in range(sect...  5.08 us
    pallas_call x1, Pallas kernels, pack(): pl.pallas_call(pack_kernel, grid=(rows // part,), in_specs=[block], out_s...  4.22 us
    pallas_call x1, Pallas kernels, finish(): pl.pallas_call(functools.partial(finish_kernel, count), grid=(steps,), in...  3.28 us
  transfers between devices with their start and end apart: 11, of which 8 were waited for; matrix products, arithmetic and copies ran while one was open for 1% of the time, Pallas kernels for 32%

profile of v4, /device:TPU:16, one launch (start us, length us, event | category | flops | bytes accessed | tf_op | source)
XLA Modules:
  0.0 138.9 jit_solution(14123841434667887772)
XLA Ops:
  0.6 0.5 collective-permute-start.10
  1.1 27.9 %shard_map.85 = (bf16[2,128,2048]{2,1,0:T(8,128)(2,1)}, bf16[2,128,2048]{2,1,0:T(8,128)(2,1)}, bf16[2,128,2048]{2,1,0:T(8,128)(2,1)}, bf16[2,128,2048]{2,1,0:T(8...) custom-call(s32[1]{0:T(128)} %bitcast.1.low_ref, ...), custom_call_target="tpu_custom_call" | custom-call | flops 1000000 | bytes 100000 | tf_op jit(solution)/shard_map/pallas_call | solution.py:100
  29.1 0.1 collective-permute-start.3
  29.2 0.5 collective-permute-start.2
  29.7 0.1 collective-permute-start.1
  29.8 0.4 collective-permute-start
  30.2 2.0 %collective-permute-done.3 = bf16[2,128,2048]{2,1,0:T(8,128)(2,1)} collective-permute-done((bf16[2,128,2048]{2,1,0:T(8,128)(2,1)}, bf16[2,128,2048]{2,1,0:T(8,128)(2,1)}, u32[]{:S(2)}, u32[]{:S(2)}) %collective-permute-start.3) | collective-permute-done | bytes 1048608 | tf_op jit(solution)/shard_map/ppermute | solution.py:154
  32.2 1.6 %copy-done.3 = f32[2,128,2048]{2,1,0:T(8,128)S(1)} copy-done((f32[2,128,2048]{2,1,0:T(8,128)S(1)}, f32[2,128,2048]{2,1,0:T(8,128)}, u32[]{:S(2)}) %copy-start.3) | copy-done | bytes 2097176
  33.8 2.3 %shard_map.89 = (bf16[1,128,2048]{2,1,0:T(8,128)(2,1)S(1)}, f32[1,128,2048]{2,1,0:T(8,128)S(1)}) custom-call(s32[1]{0:T(128)} %bitcast.own_ref, f32[1,2,128,2048]{3,2,1,0:T(8,128)S(1)} %bitcast.32, bf16[1,2,128,2048]{3,2,1,0:T(8,128)(2,1)} %bitcast.16.arrived_ref), custom_call_target="tpu_custom_call" | custom-call | flops 1000000 | bytes 100000 | tf_op jit(solution)/shard_map/pallas_call | solution.py:173
  36.1 0.0 copy-start.1
  36.1 1.6 %collective-permute-start.7 = (bf16[1,128,2048]{2,1,0:T(8,128)(2,1)S(1)}, bf16[1,128,2048]{2,1,0:T(8,128)(2,1)S(1)}, u32[]{:S(2)}, u32[]{:S(2)}) collective-permute-start(bf16[1,128,2048]{2,1,0:T(8,128)(2,1)S(1)} %get-tuple-element.38), channel_id=1, source_target_pairs={{0,4},{2,6},{4,0},{6,2},{1,5},{3,7},{5,1},{7,3},{8,12},{10,14},{12... | collective-permute-start | bytes 1572872 | tf_op jit(solution)/shard_map/ppermute | solution.py:154
  37.7 2.3 %shard_map.88 = (bf16[1,128,2048]{2,1,0:T(8,128)(2,1)S(1)}, f32[1,128,2048]{2,1,0:T(8,128)S(1)}) custom-call(s32[1]{0:T(128)} %bitcast.own_ref, f32[1,2,128,2048]{3,2,1,0:T(8,128)S(1)} %bitcast.31, bf16[1,2,128,2048]{3,2,1,0:T(8,128)(2,1)} %bitcast.13.arrived_ref), custom_call_target="tpu_custom_call" | custom-call | flops 1000000 | bytes 100000 | tf_op jit(solution)/shard_map/pallas_call | solution.py:173
  39.9 0.0 copy-start
  40.0 0.6 collective-permute-start.6
  40.6 2.3 %shard_map.87 = (bf16[1,128,2048]{2,1,0:T(8,128)(2,1)S(1)}, f32[1,128,2048]{2,1,0:T(8,128)S(1)}) custom-call(s32[1]{0:T(128)} %bitcast.own_ref, f32[1,2,128,2048]{3,2,1,0:T(8,128)S(1)} %bitcast.30, bf16[1,2,128,2048]{3,2,1,0:T(8,128)(2,1)} %bitcast.10.arrived_ref), custom_call_target="tpu_custom_call" | custom-call | flops 1000000 | bytes 100000 | tf_op jit(solution)/shard_map/pallas_call | solution.py:173
  42.9 1.6 %collective-permute-start.5 = (bf16[1,128,2048]{2,1,0:T(8,128)(2,1)S(1)}, bf16[1,128,2048]{2,1,0:T(8,128)(2,1)S(1)}, u32[]{:S(2)}, u32[]{:S(2)}) collective-permute-start(bf16[1,128,2048]{2,1,0:T(8,128)(2,1)S(1)} %get-tuple-element.36), channel_id=1, source_target_pairs={{0,4},{2,6},{4,0},{6,2},{1,5},{3,7},{5,1},{7,3},{8,12},{10,14},{12... | collective-permute-start | bytes 1572872 | tf_op jit(solution)/shard_map/ppermute | solution.py:154
  44.4 0.6 shard_map.86
  45.0 0.6 collective-permute-start.4
  45.6 5.3 %collective-permute-done.7 = bf16[1,128,2048]{2,1,0:T(8,128)(2,1)S(1)} collective-permute-done((bf16[1,128,2048]{2,1,0:T(8,128)(2,1)S(1)}, bf16[1,128,2048]{2,1,0:T(8,128)(2,1)S(1)}, u32[]{:S(2)}, u32[]{:S(2)}) %collective-permute-start.7) | collective-permute-done | bytes 524320 | tf_op jit(solution)/shard_map/ppermute | solution.py:154
  50.9 11.2 %collective-permute-done.6 = bf16[1,128,2048]{2,1,0:T(8,128)(2,1)S(1)} collective-permute-done((bf16[1,128,2048]{2,1,0:T(8,128)(2,1)S(1)}, bf16[1,128,2048]{2,1,0:T(8,128)(2,1)S(1)}, u32[]{:S(2)}, u32[]{:S(2)}) %collective-permute-start.6) | collective-permute-done | bytes 524320 | tf_op jit(solution)/shard_map/ppermute | solution.py:154
  62.1 11.2 %collective-permute-done.5 = bf16[1,128,2048]{2,1,0:T(8,128)(2,1)S(1)} collective-permute-done((bf16[1,128,2048]{2,1,0:T(8,128)(2,1)S(1)}, bf16[1,128,2048]{2,1,0:T(8,128)(2,1)S(1)}, u32[]{:S(2)}, u32[]{:S(2)}) %collective-permute-start.5) | collective-permute-done | bytes 524320 | tf_op jit(solution)/shard_map/ppermute | solution.py:154
  73.4 10.4 %collective-permute-done.4 = bf16[1,128,2048]{2,1,0:T(8,128)(2,1)S(1)} collective-permute-done((bf16[1,128,2048]{2,1,0:T(8,128)(2,1)S(1)}, bf16[1,128,2048]{2,1,0:T(8,128)(2,1)S(1)}, u32[]{:S(2)}, u32[]{:S(2)}) %collective-permute-start.4) | collective-permute-done | bytes 524320 | tf_op jit(solution)/shard_map/ppermute | solution.py:154
  83.8 3.3 %shard_map.90 = (bf16[112,8192]{1,0:T(8,128)(2,1)}, bf16[16,8192]{1,0:T(8,128)(2,1)S(1)}) custom-call(f32[128,2048]{1,0:T(8,128)S(1)} %bitcast.38, f32[128,2048]{1,0:T(8,128)S(1)} %bitcast.37, f32[128,2048]{1,0:T(8,128)S(1)} %bitcast.36, f32[128,2048]{1,0:T(8,128)S(1)} %bitcast.35, bf16[128,2048]{1,0:T(8,128)(2,1)S(1)} %bitcast.42, ...), custom_call_target="tpu_custom_call" | custom-call | flops 1000000 | bytes 100000 | tf_op jit(solution)/shard_map/pallas_call | solution.py:214
  87.1 3.2 %collective-permute-start.8 = (bf16[112,8192]{1,0:T(8,128)(2,1)}, bf16[112,8192]{1,0:T(8,128)(2,1)S(1)}, u32[]{:S(2)}, u32[]{:S(2)}) collective-permute-start(bf16[112,8192]{1,0:T(8,128)(2,1)} %get-tuple-element.39), channel_id=1, source_target_pairs={{0,8},{8,16},{16,24},{1,9},{9,17},{17,25},{2,10},{10,18},{18,26},{... | collective-permute-start | bytes 5505032 | tf_op jit(solution)/shard_map/ppermute | solution.py:278
  90.3 1.9 %collective-permute-start.9 = (bf16[16,8192]{1,0:T(8,128)(2,1)S(1)}, bf16[16,8192]{1,0:T(8,128)(2,1)S(1)}, u32[]{:S(2)}, u32[]{:S(2)}) collective-permute-start(bf16[16,8192]{1,0:T(8,128)(2,1)S(1)} %get-tuple-element.40), channel_id=1, source_target_pairs={{0,8},{8,16},{16,24},{1,9},{9,17},{17,25},{2,10},{10,18},{18,26},{... | collective-permute-start | bytes 786440 | tf_op jit(solution)/shard_map/ppermute | solution.py:278
  92.2 2.3 %collective-permute-done.10 = bf16[1,128,8192]{2,1,0:T(8,128)(2,1)} collective-permute-done((bf16[1,128,8192]{2,1,0:T(8,128)(2,1)}, bf16[1,128,8192]{2,1,0:T(8,128)(2,1)}, u32[]{:S(2)}, u32[]{:S(2)}) %collective-permute-start.10) | collective-permute-done | bytes 2097184 | tf_op jit(solution)/shard_map/ppermute | solution.py:263
  94.5 4.2 %shard_map.92 = (bf16[128,8192]{1,0:T(8,128)(2,1)}, f32[128,1]{1,0:T(8,128)}) custom-call(bf16[128,8192]{1,0:T(8,128)(2,1)} %bitcast.25.value_ref), custom_call_target="tpu_custom_call" | custom-call | flops 40000000000 | bytes 1000000 | tf_op jit(solution)/shard_map/pallas_call | solution.py:138
  98.7 1.5 %reduce = f32[128]{0:T(128)} reduce(f32[128,1]{1,0:T(8,128)} %get-tuple-element.42, f32[]{:T(128)} %constant.19), dimensions={1}, to_apply=%get-tuple-element.42.reduce_sub_computation | reduce | bytes 1028 | tf_op jit(solution)/shard_map/pallas_call | solution.py:138
  100.2 33.5 %collective-permute-done.8.part_ref = bf16[112,8192]{1,0:T(8,128)(2,1)S(1)} collective-permute-done((bf16[112,8192]{1,0:T(8,128)(2,1)}, bf16[112,8192]{1,0:T(8,128)(2,1)S(1)}, u32[]{:S(2)}, u32[]{:S(2)}) %collective-permute-start.8) | collective-permute-done | bytes 1835040 | tf_op jit(solution)/shard_map/ppermute | solution.py:278
  133.7 1.2 shard_map.91
  134.9 3.2 %collective-permute-done.9 = bf16[16,8192]{1,0:T(8,128)(2,1)S(1)} collective-permute-done((bf16[16,8192]{1,0:T(8,128)(2,1)S(1)}, bf16[16,8192]{1,0:T(8,128)(2,1)S(1)}, u32[]{:S(2)}, u32[]{:S(2)}) %collective-permute-start.9) | collective-permute-done | bytes 262176 | tf_op jit(solution)/shard_map/ppermute | solution.py:278
  138.2 0.7 bitcast_dynamic-update-slice_fusion
  (10 shorter events, 0.0 us)
Async XLA Ops:
  0.6 93.8 %collective-permute-start.10 = (bf16[1,128,8192]{2,1,0:T(8,128)(2,1)}, bf16[1,128,8192]{2,1,0:T(8,128)(2,1)}, u32[]{:S(2)}, u32[]{:S(2)}) collective-permute-start(bf16[1,128,8192]{2,1,0:T(8,128)(2,1)} %param.10), channel_id=1, source_target_pairs={{0,24},{8,16},{16,8},{24,0},{1,25},{9,17},{17,9},{25,1},{2,26},{10... | collective-permute-start | bytes 6291464 | tf_op jit(solution)/shard_map/ppermute | solution.py:263
  29.1 8.6 %copy-start.2 = (f32[2,128,2048]{2,1,0:T(8,128)S(1)}, f32[2,128,2048]{2,1,0:T(8,128)}, u32[]{:S(2)}) copy-start(f32[2,128,2048]{2,1,0:T(8,128)} %get-tuple-element.29) | copy-start | bytes 6291460
  29.1 3.1 %collective-permute-start.3 = (bf16[2,128,2048]{2,1,0:T(8,128)(2,1)}, bf16[2,128,2048]{2,1,0:T(8,128)(2,1)}, u32[]{:S(2)}, u32[]{:S(2)}) collective-permute-start(bf16[2,128,2048]{2,1,0:T(8,128)(2,1)} %get-tuple-element.33), channel_id=1, source_target_pairs={{0,2},{2,0},{4,6},{6,4},{1,3},{3,1},{5,7},{7,5},{8,10},{10,8},{12,... | collective-permute-start | bytes 3145736 | tf_op jit(solution)/shard_map/ppermute | solution.py:154
  29.2 8.5 %collective-permute-start.2 = (bf16[2,128,2048]{2,1,0:T(8,128)(2,1)}, bf16[2,128,2048]{2,1,0:T(8,128)(2,1)}, u32[]{:S(2)}, u32[]{:S(2)}) collective-permute-start(bf16[2,128,2048]{2,1,0:T(8,128)(2,1)} %get-tuple-element.30), channel_id=1, source_target_pairs={{0,2},{2,0},{4,6},{6,4},{1,3},{3,1},{5,7},{7,5},{8,10},{10,8},{12,... | collective-permute-start | bytes 3145736 | tf_op jit(solution)/shard_map/ppermute | solution.py:154
  29.7 10.9 %collective-permute-start.1 = (bf16[2,128,2048]{2,1,0:T(8,128)(2,1)}, bf16[2,128,2048]{2,1,0:T(8,128)(2,1)}, u32[]{:S(2)}, u32[]{:S(2)}) collective-permute-start(bf16[2,128,2048]{2,1,0:T(8,128)(2,1)} %get-tuple-element.27), channel_id=1, source_target_pairs={{0,2},{2,0},{4,6},{6,4},{1,3},{3,1},{5,7},{7,5},{8,10},{10,8},{12,... | collective-permute-start | bytes 3145736 | tf_op jit(solution)/shard_map/ppermute | solution.py:154
  29.8 14.7 %collective-permute-start = (bf16[2,128,2048]{2,1,0:T(8,128)(2,1)}, bf16[2,128,2048]{2,1,0:T(8,128)(2,1)S(1)}, u32[]{:S(2)}, u32[]{:S(2)}) collective-permute-start(bf16[2,128,2048]{2,1,0:T(8,128)(2,1)} %get-tuple-element.24), channel_id=1, source_target_pairs={{0,2},{2,0},{4,6},{6,4},{1,3},{3,1},{5,7},{7,5},{8,10},{10,8},{12,... | collective-permute-start | bytes 3145736 | tf_op jit(solution)/shard_map/ppermute | solution.py:154
  32.2 1.6 %copy-start.3 = (f32[2,128,2048]{2,1,0:T(8,128)S(1)}, f32[2,128,2048]{2,1,0:T(8,128)}, u32[]{:S(2)}) copy-start(f32[2,128,2048]{2,1,0:T(8,128)} %get-tuple-element.32) | copy-start | bytes 6291460
  36.1 4.5 %copy-start.1 = (f32[2,128,2048]{2,1,0:T(8,128)S(1)}, f32[2,128,2048]{2,1,0:T(8,128)}, u32[]{:S(2)}) copy-start(f32[2,128,2048]{2,1,0:T(8,128)} %get-tuple-element.26) | copy-start | bytes 6291460
  36.1 14.8 %collective-permute-start.7 = (bf16[1,128,2048]{2,1,0:T(8,128)(2,1)S(1)}, bf16[1,128,2048]{2,1,0:T(8,128)(2,1)S(1)}, u32[]{:S(2)}, u32[]{:S(2)}) collective-permute-start(bf16[1,128,2048]{2,1,0:T(8,128)(2,1)S(1)} %get-tuple-element.38), channel_id=1, source_target_pairs={{0,4},{2,6},{4,0},{6,2},{1,5},{3,7},{5,1},{7,3},{8,12},{10,14},{12... | collective-permute-start | bytes 1572872 | tf_op jit(solution)/shard_map/ppermute | solution.py:154
  39.9 4.5 %copy-start = (f32[2,128,2048]{2,1,0:T(8,128)S(1)}, f32[2,128,2048]{2,1,0:T(8,128)}, u32[]{:S(2)}) copy-start(f32[2,128,2048]{2,1,0:T(8,128)} %get-tuple-element.23) | copy-start | bytes 6291460
  40.0 22.2 %collective-permute-start.6 = (bf16[1,128,2048]{2,1,0:T(8,128)(2,1)S(1)}, bf16[1,128,2048]{2,1,0:T(8,128)(2,1)S(1)}, u32[]{:S(2)}, u32[]{:S(2)}) collective-permute-start(bf16[1,128,2048]{2,1,0:T(8,128)(2,1)S(1)} %get-tuple-element.37), channel_id=1, source_target_pairs={{0,4},{2,6},{4,0},{6,2},{1,5},{3,7},{5,1},{7,3},{8,12},{10,14},{12... | collective-permute-start | bytes 1572872 | tf_op jit(solution)/shard_map/ppermute | solution.py:154
  42.9 41.0 %copy-start.4 = (bf16[1,128,8192]{2,1,0:T(8,128)(2,1)S(1)}, bf16[1,128,8192]{2,1,0:T(8,128)(2,1)}, u32[]{:S(2)}) copy-start(bf16[1,128,8192]{2,1,0:T(8,128)(2,1)} %param.10) | copy-start | bytes 6291460
  42.9 30.5 %collective-permute-start.5 = (bf16[1,128,2048]{2,1,0:T(8,128)(2,1)S(1)}, bf16[1,128,2048]{2,1,0:T(8,128)(2,1)S(1)}, u32[]{:S(2)}, u32[]{:S(2)}) collective-permute-start(bf16[1,128,2048]{2,1,0:T(8,128)(2,1)S(1)} %get-tuple-element.36), channel_id=1, source_target_pairs={{0,4},{2,6},{4,0},{6,2},{1,5},{3,7},{5,1},{7,3},{8,12},{10,14},{12... | collective-permute-start | bytes 1572872 | tf_op jit(solution)/shard_map/ppermute | solution.py:154
  45.0 38.8 %collective-permute-start.4 = (bf16[1,128,2048]{2,1,0:T(8,128)(2,1)S(1)}, bf16[1,128,2048]{2,1,0:T(8,128)(2,1)S(1)}, u32[]{:S(2)}, u32[]{:S(2)}) collective-permute-start(bf16[1,128,2048]{2,1,0:T(8,128)(2,1)S(1)} %get-tuple-element.35), channel_id=1, source_target_pairs={{0,4},{2,6},{4,0},{6,2},{1,5},{3,7},{5,1},{7,3},{8,12},{10,14},{12... | collective-permute-start | bytes 1572872 | tf_op jit(solution)/shard_map/ppermute | solution.py:154
  87.1 46.6 %collective-permute-start.8 = (bf16[112,8192]{1,0:T(8,128)(2,1)}, bf16[112,8192]{1,0:T(8,128)(2,1)S(1)}, u32[]{:S(2)}, u32[]{:S(2)}) collective-permute-start(bf16[112,8192]{1,0:T(8,128)(2,1)} %get-tuple-element.39), channel_id=1, source_target_pairs={{0,8},{8,16},{16,24},{1,9},{9,17},{17,25},{2,10},{10,18},{18,26},{... | collective-permute-start | bytes 5505032 | tf_op jit(solution)/shard_map/ppermute | solution.py:278
  90.3 47.9 %collective-permute-start.9 = (bf16[16,8192]{1,0:T(8,128)(2,1)S(1)}, bf16[16,8192]{1,0:T(8,128)(2,1)S(1)}, u32[]{:S(2)}, u32[]{:S(2)}) collective-permute-start(bf16[16,8192]{1,0:T(8,128)(2,1)S(1)} %get-tuple-element.40), channel_id=1, source_target_pairs={{0,8},{8,16},{16,24},{1,9},{9,17},{17,25},{2,10},{10,18},{18,26},{... | collective-permute-start | bytes 786440 | tf_op jit(solution)/shard_map/ppermute | solution.py:278
